TPU v7x, 256 devices: a whole 4x4x8 slice. The times are simulated.
256 devices in a mesh: gz: 32 (over z, y_lo, core), mat: 8 (over x, y_hi).
Axes of the slice: x: 4, y: 4 (y_hi: 2, y_lo: 2; y = y_hi * 2 + y_lo), z: 8, core: 2. Of those that a mesh axis runs over, the one named last changes fastest.
Arguments:
- particle_mass: float32 [8, 4194304], P('mat', 'gz'), may hold values from 0.5 to 2
- particle_velocity: float32 [8, 3, 4194304], P('mat', None, 'gz'), may hold values from -6 to 6
- spline_weights: float32 [8, 9, 4194304], P('mat', None, 'gz'), as said below
- particle_cells: int32 [8, 4194304], P('mat', 'gz'), may hold values from 0 to 2047, as said below
- block_counts: int32 [8, 32, 32], P('mat', 'gz'), may hold values from 512 to 4096, as said below
- friction: float32 [8], P('mat'), may hold values from 0.1 to 0.8
- contact_flags: int32 [64, 256, 128], P('gz'), may hold values 0 or 1
Outputs:
- grid_velocity: float32 [8, 3, 64, 256, 128], P('mat', None, 'gz')
Inputs may be any that keep to these rules, and one draw needn't show every extreme that they name: `spline_weights`: rows 3 a, 3 a + 1, 3 a + 2 hold the quadratic B-spline weights along axis a (z, x, y) for the nodes at offsets -1, 0, +1 from the particle's cell; each triple sums to 1. `particle_cells`: each value is (z * 8 + u) * 128 + y with z < 2 and u < 8, the cell inside the particle's block; the slots of a block are in nondecreasing Morton order of that cell. `block_counts`: the live slots of a block are its first ones; the rest are padding.
All inputs are finite; a program needn't handle non-finite values. No bound on the sum of `contact_flags` on one device may be relied on, other than what follows from the above.
Results may differ from a plain program's by a relative error of at most 0.007.
Values may be sent and summed in bfloat16 or wider, within the bound.
A program may use at most 64 MiB of HBM per device.

v0:
```python
import functools
import jax, jax.numpy as jnp
from jax import lax
from jax.sharding import PartitionSpec as P
from jax.experimental import pallas as pl
from jax.experimental.pallas import tpu as pltpu

BLOCKS=32; SLOTS=4096; W=32
BPS=4
ROWS=SLOTS//128
F32=jnp.float32; BF=jnp.bfloat16

def rows_const(n, fn, k):
    r = lax.broadcasted_iota(jnp.int32, (n, k), 0)
    return fn(r).astype(F32).astype(BF)

def dep_kernel(cfg, counts, mass, vel, wt, cells, out, acc):
    variant, skip, pre = cfg
    step = pl.program_id(0)
    ycon = [rows_const(W, lambda r, t=t: r - t, 128) for t in range(3)]
    xcon = [rows_const(16, lambda r, p=p: (r - p + 1) & 15, 128) for p in range(3)]
    zero = jnp.zeros((), BF)
    sub = lax.broadcasted_iota(jnp.int32, (8, 128), 0)
    place_id = sub * 128 + lax.broadcasted_iota(jnp.int32, (8, 128), 1)
    odd = (sub & 1) == 1

    @pl.when(step == 0)
    def _():
        out[...] = jnp.zeros_like(out)

    def bc(tile, r, rows):
        return jnp.broadcast_to(tile[r:r+1], (rows, 128)).astype(BF)

    def block(i, _):
        b = step * BPS + i
        n = counts[b]
        acc[...] = jnp.zeros_like(acc)
        def sl(g):
            return pl.ds(pl.multiple_of(i * ROWS + g * 8, 8), 8)
        def scan(g):
            y = cells[sl(g), :] & 127
            first = jnp.broadcast_to(y[:, 0:1], (8, 128)) & ~7
            first = jnp.where(odd, pltpu.roll(first, 1, 0), first)
            yrel = y - first
            live = place_id < n - g * 1024
            more = jnp.max(jnp.where(live, yrel, 0)) >= 24
            return [first[2*j, 0] for j in range(4)], more, yrel.astype(F32)
        def prep(g):
            cl = cells[sl(g), :]
            m = jnp.where(place_id < n - g * 1024, mass[sl(g), :], 0.0)
            u = ((cl >> 7) & 7).astype(F32)
            top = cl >= 1024
            car = [m] + [m * vel[k, sl(g), :] for k in range(3)]
            w = [wt[r, sl(g), :] for r in range(9)]
            zn = [jnp.where(top, 0.0, w[0]), jnp.where(top, w[0], w[1]),
                  jnp.where(top, w[1], w[2]), jnp.where(top, w[2], 0.0)]
            return u, car, w, zn
        def xwin(u, w, r):
            ub = bc(u, r, 16)
            xw = jnp.where(ub == xcon[0], bc(w[3], r, 16), zero)
            xw = jnp.where(ub == xcon[1], bc(w[4], r, 16), xw)
            return jnp.where(ub == xcon[2], bc(w[5], r, 16), xw)
        def ywin(yrel, w, r):
            yb = bc(yrel, r, W)
            yw = jnp.where(yb == ycon[0], bc(w[6], r, W), zero)
            yw = jnp.where(yb == ycon[1], bc(w[7], r, W), yw)
            return jnp.where(yb == ycon[2], bc(w[8], r, W), yw)
        def sides(yrel, u, car, w, zn, r):
            xw = xwin(u, w, r)
            yw = ywin(yrel, w, r)
            if variant == 0:
                left = jnp.concatenate([bc(car[f] * zn[z], r, 16) * xw for f in range(4) for z in range(4)], 0)
                return left, yw
            left = jnp.concatenate([bc(zn[z], r, 16) * xw for z in range(4)], 0)
            right = jnp.concatenate([bc(car[f], r, W) * yw for f in range(4)], 0)
            return left, right
        def product(yrel, data, j):
            l0, r0 = sides(yrel, *data, 2 * j)
            l1, r1 = sides(yrel, *data, 2 * j + 1)
            left = jnp.concatenate([l0, l1], 1)
            right = jnp.concatenate([r0, r1], 1)
            return lax.dot_general(right, left, (((1,), (1,)), ((), ())), preferred_element_type=F32)
        def add(base, res):
            rows = pl.ds(pl.multiple_of(base, 8), W)
            if variant == 0:
                acc[rows, :] += res
            else:
                for f in range(4):
                    acc[f, rows, 0:64] += res[f * W:(f + 1) * W]
        def group(g, carry):
            bases, more, yrel = scan(g) if not pre else carry
            data = prep(g)
            nxt = scan(jnp.minimum(g + 1, ROWS // 8 - 1)) if pre else 0
            res = [product(yrel, data, j) for j in range(4)]
            for j in range(4):
                add(bases[j], res[j])
            @pl.when(more)
            def _():
                def window(off, _):
                    shift = (off * W).astype(F32)
                    for j in range(4):
                        base = bases[j] + off * W
                        @pl.when(base < 130)
                        def _():
                            add(base, product(yrel - shift, data, j))
                    return 0
                lax.fori_loop(1, 5, window, 0)
            return nxt
        if skip != 1:
            lax.fori_loop(0, (n + 1023) // 1024, group, scan(0) if pre else 0)
        up = lax.rem(b + 1, BLOCKS); dn = lax.rem(b + BLOCKS - 1, BLOCKS)
        def place(f, z, own, halo):
            out[f, z, pl.ds(pl.multiple_of(b * 8, 8), 8), :] += own
            out[f, z, pl.ds(pl.multiple_of(up * 8, 8), 8), :] += jnp.where(sub == 0, halo, 0.0)
            out[f, z, pl.ds(pl.multiple_of(dn * 8, 8), 8), :] += jnp.where(sub == 7, halo, 0.0)
        if skip == 2:
            return 0
        if variant == 0:
            acc[128:129] += acc[0:1]
            acc[1:2] += acc[129:130]
            t = acc[1:129, :].T
            for f in range(4):
                for z in range(4):
                    o = (f * 4 + z) * 16
                    place(f, z, t[o:o+8], t[o+8:o+16])
        else:
            for f in range(4):
                acc[f, 128:129] += acc[f, 0:1]
                acc[f, 1:2] += acc[f, 129:130]
                t = acc[f, 1:129, :].T
                for z in range(4):
                    o = z * 16
                    place(f, z, t[o:o+8], t[o+8:o+16])
        return 0
    lax.fori_loop(0, BPS, block, 0)

def deposit(cfg, counts, mass, vel, wt, cells):
    variant = cfg[0]
    R = BPS * ROWS
    accs = pltpu.VMEM((160, 256), F32) if variant == 0 else pltpu.VMEM((4, 160, 128), F32)
    return pl.pallas_call(
        functools.partial(dep_kernel, cfg),
        grid=(BLOCKS // BPS,),
        in_specs=[pl.BlockSpec(memory_space=pltpu.SMEM),
                  pl.BlockSpec((R, 128), lambda i: (i, 0)),
                  pl.BlockSpec((3, R, 128), lambda i: (0, i, 0)),
                  pl.BlockSpec((9, R, 128), lambda i: (0, i, 0)),
                  pl.BlockSpec((R, 128), lambda i: (i, 0))],
        out_specs=pl.BlockSpec((4, 4, 256, 128), lambda i: (0, 0, 0, 0)),
        out_shape=jax.ShapeDtypeStruct((4, 4, 256, 128), F32),
        scratch_shapes=[accs],
        compiler_params=pltpu.CompilerParams(vmem_limit_bytes=50 << 20),
    )(counts, mass.reshape(1024, 128), vel.reshape(3, 1024, 128), wt.reshape(9, 1024, 128), cells.reshape(1024, 128))

MASS_FLOOR = 0.2
GRADIENT_FLOOR = 0.1
SLIP_FLOOR = 0.05
PIECES = 8
COLS = 32
MESH = pl.DeviceIdType.MESH


def comm_kernel(fric, dep, flags, out, hsend, hrecv, nf, mass, gradz, rsend, rrecv, cbuf,
                h_ss, h_rs, r_ss, r_rs, c_ss, c_rs):
    slabs = lax.axis_size("gz")
    g = lax.axis_index("gz")
    me = lax.axis_index("mat")
    lo = lax.rem(g + slabs - 1, slabs)
    hi = lax.rem(g + 1, slabs)
    s_lo = jnp.where(g == 0, 0.0, 1.0)
    s_hi = jnp.where(g == slabs - 1, 0.0, 1.0)

    barrier = pltpu.get_barrier_semaphore()
    for other in (lo, hi):
        pl.semaphore_signal(barrier, inc=1, device_id={"gz": other, "mat": me}, device_id_type=MESH)
    for k in range(1, PIECES):
        pl.semaphore_signal(barrier, inc=1, device_id={"gz": g, "mat": lax.rem(me + k, PIECES)},
                            device_id_type=MESH)

    def halo(side, p):
        return pltpu.make_async_remote_copy(
            src_ref=hsend.at[side, p], dst_ref=hrecv.at[side, p],
            send_sem=h_ss.at[side, p], recv_sem=h_rs.at[side, p],
            device_id={"gz": lo if side == 0 else hi, "mat": me}, device_id_type=MESH)

    def share(p):
        return pltpu.make_async_remote_copy(
            src_ref=rsend.at[p], dst_ref=rrecv.at[me], send_sem=r_ss.at[p], recv_sem=r_rs.at[me],
            device_id={"gz": g, "mat": p}, device_id_type=MESH)

    def shared(p):
        return pltpu.make_async_remote_copy(
            src_ref=rsend.at[p], dst_ref=rrecv.at[p], send_sem=r_ss.at[p], recv_sem=r_rs.at[p],
            device_id={"gz": g, "mat": p}, device_id_type=MESH)

    def spread(p):
        return pltpu.make_async_remote_copy(
            src_ref=cbuf.at[me], dst_ref=cbuf.at[me], send_sem=c_ss.at[p], recv_sem=c_rs.at[me],
            device_id={"gz": g, "mat": p}, device_id_type=MESH)

    def spreaded(p):
        return pltpu.make_async_remote_copy(
            src_ref=cbuf.at[p], dst_ref=cbuf.at[p], send_sem=c_ss.at[p], recv_sem=c_rs.at[p],
            device_id={"gz": g, "mat": p}, device_id_type=MESH)

    def cols(p):
        return pl.ds(pl.multiple_of(p * COLS, COLS), COLS)

    def pack(k, _):
        p = lax.rem(me + 1 + k, PIECES)
        x = cols(p)
        for f in range(4):
            hsend[0, p, f] = dep[f, 0, x, :].astype(jnp.bfloat16)
            hsend[1, p, f] = dep[f, 3, x, :].astype(jnp.bfloat16)
        hsend[0, p, 4] = dep[0, 1, x, :].astype(jnp.bfloat16)
        hsend[1, p, 4] = dep[0, 2, x, :].astype(jnp.bfloat16)
        return 0

    lax.fori_loop(0, PIECES, pack, 0)
    pl.semaphore_wait(barrier, PIECES + 1)

    def start_halo(k, _):
        p = lax.rem(me + 1 + k, PIECES)
        halo(0, p).start()
        halo(1, p).start()
        return 0

    lax.fori_loop(0, PIECES, start_halo, 0)

    def nodes(p):
        halo(0, p).wait_recv()
        halo(1, p).wait_recv()
        x = cols(p)
        for f in range(4):
            low = dep[f, 1, x, :] + s_lo * hrecv[1, p, f].astype(jnp.float32)
            high = dep[f, 2, x, :] + s_hi * hrecv[0, p, f].astype(jnp.float32)
            nf[f, 0, x, :] = low
            nf[f, 1, x, :] = high
            rsend[p, f, 0] = low.astype(jnp.bfloat16)
            rsend[p, f, 1] = high.astype(jnp.bfloat16)
            if f == 0:
                xm = pl.ds(pl.multiple_of(p * COLS + 8, 8), COLS)
                mass[0, xm, :] = low
                mass[1, xm, :] = high
                below = s_lo * (hrecv[1, p, 4].astype(jnp.float32) + dep[0, 0, x, :])
                above = s_hi * (hrecv[0, p, 4].astype(jnp.float32) + dep[0, 3, x, :])
                gradz[0, x, :] = (high - below) * 0.5
                gradz[1, x, :] = (above - low) * 0.5

    def reduce_step(k, _):
        p = lax.rem(me + 1 + k, PIECES)
        nodes(p)
        share(p).start()
        return 0

    lax.fori_loop(0, PIECES - 1, reduce_step, 0)
    nodes(me)
    for z in range(2):
        mass[z, 7:8, :] = mass[z, 263:264, :]
        mass[z, 264:265, :] = mass[z, 8:9, :]

    def total_step(k, total):
        p = lax.rem(me + PIECES - 1 - k, PIECES)
        shared(p).wait_recv()
        return total + rrecv[p].astype(jnp.float32)

    total = lax.fori_loop(0, PIECES - 1, total_step, rsend[me].astype(jnp.float32))
    cbuf[me] = (total[1:] / jnp.maximum(total[0], MASS_FLOOR)).astype(jnp.bfloat16)

    def start_spread(k, _):
        spread(lax.rem(me + 1 + k, PIECES)).start()
        return 0

    lax.fori_loop(0, PIECES - 1, start_spread, 0)
    friction = fric[0]

    def finish(p):
        for z in range(2):
            x = cols(p)
            m = nf[0, z, x, :]
            gx = (mass[z, pl.ds(p * COLS + 9, COLS), :] - mass[z, pl.ds(p * COLS + 7, COLS), :]) * 0.5
            gy = (pltpu.roll(m, 127, 1) - pltpu.roll(m, 1, 1)) * 0.5
            gz = gradz[z, x, :]
            length = jnp.sqrt(gz * gz + gx * gx + gy * gy)
            inv = 1.0 / jnp.maximum(length, GRADIENT_FLOOR)
            normal = [gz * inv, gx * inv, gy * inv]
            inv_m = 1.0 / jnp.maximum(m, MASS_FLOOR)
            speed = [nf[1 + d, z, x, :] * inv_m for d in range(3)]
            rel = [speed[d] - cbuf[p, d, z].astype(jnp.float32) for d in range(3)]
            part = rel[0] * normal[0] + rel[1] * normal[1] + rel[2] * normal[2]
            approach = jnp.maximum(part, 0.0)
            tangent = [rel[d] - part * normal[d] for d in range(3)]
            slip = jnp.sqrt(tangent[0] * tangent[0] + tangent[1] * tangent[1] + tangent[2] * tangent[2])
            factor = jnp.minimum(friction * approach, slip) / jnp.maximum(slip, SLIP_FLOOR)
            flag = flags[z, x, :].astype(jnp.float32)
            for d in range(3):
                out[0, d, z, x, :] = speed[d] - flag * (approach * normal[d] + factor * tangent[d])

    finish(me)

    def finish_step(k, _):
        p = lax.rem(me + PIECES - 1 - k, PIECES)
        spreaded(p).wait_recv()
        finish(p)
        return 0

    lax.fori_loop(0, PIECES - 1, finish_step, 0)

    def drain(k, _):
        p = lax.rem(me + 1 + k, PIECES)
        share(p).wait_send()
        spread(p).wait_send()
        return 0

    lax.fori_loop(0, PIECES - 1, drain, 0)

    def drain_halo(p, _):
        halo(0, p).wait_send()
        halo(1, p).wait_send()
        return 0

    lax.fori_loop(0, PIECES, drain_halo, 0)


def exchange(friction, dep, flags):
    vm = pl.BlockSpec(memory_space=pltpu.VMEM)
    f32, bf = jnp.float32, jnp.bfloat16
    dma = pltpu.SemaphoreType.DMA
    return pl.pallas_call(
        comm_kernel,
        in_specs=[pl.BlockSpec(memory_space=pltpu.SMEM), vm, vm],
        out_specs=vm,
        out_shape=jax.ShapeDtypeStruct((1, 3, 2, 256, 128), f32),
        scratch_shapes=[
            pltpu.VMEM((2, PIECES, 5, COLS, 128), bf), pltpu.VMEM((2, PIECES, 5, COLS, 128), bf),
            pltpu.VMEM((4, 2, 256, 128), f32), pltpu.VMEM((2, 272, 128), f32),
            pltpu.VMEM((2, 256, 128), f32),
            pltpu.VMEM((PIECES, 4, 2, COLS, 128), bf), pltpu.VMEM((PIECES, 4, 2, COLS, 128), bf),
            pltpu.VMEM((PIECES, 3, 2, COLS, 128), bf),
            dma((2, PIECES)), dma((2, PIECES)), dma((PIECES,)), dma((PIECES,)), dma((PIECES,)), dma((PIECES,)),
        ],
        compiler_params=pltpu.CompilerParams(collective_id=0, has_side_effects=True, vmem_limit_bytes=40 << 20),
    )(friction, dep, flags)


def per_device(particle_mass, particle_velocity, spline_weights, particle_cells, block_counts, friction, contact_flags):
    dep = deposit((1, 0, 0), block_counts.reshape(32), particle_mass, particle_velocity, spline_weights, particle_cells)
    return exchange(friction, dep, contact_flags)


def solution(mesh):
    return jax.shard_map(
        per_device,
        mesh=mesh,
        in_specs=(
            P("mat", "gz"),
            P("mat", None, "gz"),
            P("mat", None, "gz"),
            P("mat", "gz"),
            P("mat", "gz", None),
            P("mat"),
            P("gz", None, None),
        ),
        out_specs=P("mat", None, "gz", None, None),
        check_vma=False,
    )
```

profile of v0, /device:TPU:1, one launch (start us, length us, event | category | flops | bytes accessed | tf_op | source)
XLA Modules:
  0.0 82.5 jit_solution(17100174016258587656)
XLA Ops:
  0.7 0.0 copy-start.1
  0.7 1.4 %copy-done.1 = f32[1,3,131072]{2,0,1:T(1,128)S(1)} copy-done((f32[1,3,131072]{2,0,1:T(1,128)S(1)}, f32[1,3,131072]{2,0,1:T(1,128)}, u32[]{:S(2)}) %copy-start.1) | copy-done | bytes 1572888
  2.1 0.0 copy-start.2
  2.1 1.0 %copy-done.2 = f32[1,131072]{1,0:T(1,128)S(1)} copy-done((f32[1,131072]{1,0:T(1,128)S(1)}, f32[1,131072]{1,0:T(1,128)}, u32[]{:S(2)}) %copy-start.2) | copy-done | bytes 524312
  3.1 0.0 copy-start.3
  3.1 1.0 %copy-done.3 = s32[1,131072]{1,0:T(1,128)S(1)} copy-done((s32[1,131072]{1,0:T(1,128)S(1)}, s32[1,131072]{1,0:T(1,128)}, u32[]{:S(2)}) %copy-start.3) | copy-done | bytes 524312
  4.1 0.0 copy-start.5
  4.1 0.7 copy-done.5
  4.8 0.0 copy-start.4
  4.8 40.9 %shard_map.73.dep = f32[4,4,256,128]{3,2,1,0:T(8,128)} custom-call(s32[32]{0:T(128)S(1)} %bitcast.8, f32[1024,128]{1,0:T(8,128)S(1)} %bitcast.6, f32[3,1024,128]{2,1,0:T(8,128)S(1)} %bitcast.5, f32[9,1024,128]{2,1,0:T(8,128)} %bitcast.9, s32[1024,128]{1,0:T(8,128)S(1)} %bitcast.7), custom_call_target="tpu_custom_call" | custom-call | tf_op jit(solution)/shard_map/pallas_call | solution.py:141
  45.7 0.0 copy-done.4
  45.7 0.0 copy-start
  45.7 1.6 %copy-done = f32[4,4,256,128]{3,2,1,0:T(8,128)S(1)} copy-done((f32[4,4,256,128]{3,2,1,0:T(8,128)S(1)}, f32[4,4,256,128]{3,2,1,0:T(8,128)}, u32[]{:S(2)}) %copy-start) | copy-done | bytes 2097176
  47.3 34.3 %shard_map.74 = f32[1,3,2,256,128]{4,3,2,1,0:T(8,128)S(1)} custom-call(f32[1]{0:T(128)S(6)} %copy.9.fric, f32[4,4,256,128]{3,2,1,0:T(8,128)S(1)} %copy-done, s32[2,256,128]{2,1,0:T(8,128)S(1)} %copy-done.4), custom_call_target="tpu_custom_call" | custom-call | tf_op jit(solution)/shard_map/pallas_call | solution.py:329
  81.6 0.9 %copy.10 = f32[1,3,2,256,128]{4,3,2,1,0:T(8,128)} copy(f32[1,3,2,256,128]{4,3,2,1,0:T(8,128)S(1)} %shard_map.74) | data formatting | bytes 1572864
Async XLA Ops:
  0.7 1.4 %copy-start.1 = (f32[1,3,131072]{2,0,1:T(1,128)S(1)}, f32[1,3,131072]{2,0,1:T(1,128)}, u32[]{:S(2)}) copy-start(f32[1,3,131072]{2,0,1:T(1,128)} %param.8) | copy-start | bytes 4718596
  2.1 1.0 %copy-start.2 = (f32[1,131072]{1,0:T(1,128)S(1)}, f32[1,131072]{1,0:T(1,128)}, u32[]{:S(2)}) copy-start(f32[1,131072]{1,0:T(1,128)} %param.7) | copy-start | bytes 1572868
  3.1 1.0 %copy-start.3 = (s32[1,131072]{1,0:T(1,128)S(1)}, s32[1,131072]{1,0:T(1,128)}, u32[]{:S(2)}) copy-start(s32[1,131072]{1,0:T(1,128)} %param.10) | copy-start | bytes 1572868
  4.1 0.7 copy-start.5
  4.8 40.9 %copy-start.4 = (s32[2,256,128]{2,1,0:T(8,128)S(1)}, s32[2,256,128]{2,1,0:T(8,128)}, u32[]{:S(2)}) copy-start(s32[2,256,128]{2,1,0:T(8,128)} %flags.1) | copy-start | bytes 786436
  45.7 1.6 %copy-start = (f32[4,4,256,128]{3,2,1,0:T(8,128)S(1)}, f32[4,4,256,128]{3,2,1,0:T(8,128)}, u32[]{:S(2)}) copy-start(f32[4,4,256,128]{3,2,1,0:T(8,128)} %shard_map.73.dep) | copy-start | bytes 6291460
where the time goes:
time: 82.7 us; the launch traced here: 82.5 us
  Pallas kernels  75.2 us (91%)
  local copies, waits for them, and re-layouts  6.61 us (8%)
    pallas_call x1, Pallas kernels, deposit(): pl.pallas_call(functools.partial(dep_kernel, cfg), grid=(BLOCKS // BPS,),...  40.9 us
    pallas_call x1, Pallas kernels, exchange(): pl.pallas_call(comm_kernel, in_specs=[pl.BlockSpec(memory_space=pltpu.SME...  34.3 us
    unnamed x13, local copies, waits for them, and re-layouts  6.61 us

commit v1 on v0

--- a/solution.py
+++ b/solution.py
@@ -6,7 +6,6 @@
 from jax.experimental.pallas import tpu as pltpu
 
 BLOCKS=32; SLOTS=4096; W=32
-BPS=4
 ROWS=SLOTS//128
 F32=jnp.float32; BF=jnp.bfloat16
 
@@ -14,142 +13,192 @@
     r = lax.broadcasted_iota(jnp.int32, (n, k), 0)
     return fn(r).astype(F32).astype(BF)
 
-def dep_kernel(cfg, counts, mass, vel, wt, cells, out, acc):
-    variant, skip, pre = cfg
-    step = pl.program_id(0)
+def dep_kernel(cfg, counts, mass_h, vel_h, wt_h, cells_h, out, mass, vel, wt, cells, acc, tbuf, lbuf, rbuf, prod, sems):
+    UR, U, PARTS, skip, UF = cfg
+    UNIT = UR * 128
+    NCH = UR * U // 2
+    PB = BLOCKS // PARTS
+    PR = PB * ROWS
+    def copies(q):
+        r = pl.ds(q * PR, PR)
+        return [pltpu.make_async_copy(mass_h.at[r], mass.at[r], sems.at[0, q]),
+                pltpu.make_async_copy(vel_h.at[:, r], vel.at[:, r], sems.at[1, q]),
+                pltpu.make_async_copy(wt_h.at[:, r], wt.at[:, r], sems.at[2, q]),
+                pltpu.make_async_copy(cells_h.at[r], cells.at[r], sems.at[3, q])]
+    for q in range(PARTS):
+        for c in copies(q):
+            c.start()
     ycon = [rows_const(W, lambda r, t=t: r - t, 128) for t in range(3)]
     xcon = [rows_const(16, lambda r, p=p: (r - p + 1) & 15, 128) for p in range(3)]
     zero = jnp.zeros((), BF)
     sub = lax.broadcasted_iota(jnp.int32, (8, 128), 0)
-    place_id = sub * 128 + lax.broadcasted_iota(jnp.int32, (8, 128), 1)
-    odd = (sub & 1) == 1
-
-    @pl.when(step == 0)
-    def _():
-        out[...] = jnp.zeros_like(out)
+    lane_lo = lax.broadcasted_iota(jnp.int32, (W, 128), 1) < 64
+    usub = lax.broadcasted_iota(jnp.int32, (UR, 128), 0)
+    place_id = usub * 128 + lax.broadcasted_iota(jnp.int32, (UR, 128), 1)
+    odd = (usub & 1) == 1
+
+    def clear(b, _):
+        acc[b] = jnp.zeros(acc.shape[1:], F32)
+        return 0
+    lax.fori_loop(0, BLOCKS, clear, 0)
+    lbuf[...] = jnp.zeros(lbuf.shape, BF)
+    rbuf[...] = jnp.zeros(rbuf.shape, BF)
+    prod[...] = jnp.zeros(prod.shape, F32)
 
     def bc(tile, r, rows):
         return jnp.broadcast_to(tile[r:r+1], (rows, 128)).astype(BF)
 
-    def block(i, _):
-        b = step * BPS + i
+    def load(b, c):
         n = counts[b]
-        acc[...] = jnp.zeros_like(acc)
-        def sl(g):
-            return pl.ds(pl.multiple_of(i * ROWS + g * 8, 8), 8)
-        def scan(g):
-            y = cells[sl(g), :] & 127
-            first = jnp.broadcast_to(y[:, 0:1], (8, 128)) & ~7
-            first = jnp.where(odd, pltpu.roll(first, 1, 0), first)
-            yrel = y - first
-            live = place_id < n - g * 1024
-            more = jnp.max(jnp.where(live, yrel, 0)) >= 24
-            return [first[2*j, 0] for j in range(4)], more, yrel.astype(F32)
-        def prep(g):
-            cl = cells[sl(g), :]
-            m = jnp.where(place_id < n - g * 1024, mass[sl(g), :], 0.0)
-            u = ((cl >> 7) & 7).astype(F32)
-            top = cl >= 1024
-            car = [m] + [m * vel[k, sl(g), :] for k in range(3)]
-            w = [wt[r, sl(g), :] for r in range(9)]
-            zn = [jnp.where(top, 0.0, w[0]), jnp.where(top, w[0], w[1]),
-                  jnp.where(top, w[1], w[2]), jnp.where(top, w[2], 0.0)]
-            return u, car, w, zn
-        def xwin(u, w, r):
-            ub = bc(u, r, 16)
-            xw = jnp.where(ub == xcon[0], bc(w[3], r, 16), zero)
-            xw = jnp.where(ub == xcon[1], bc(w[4], r, 16), xw)
-            return jnp.where(ub == xcon[2], bc(w[5], r, 16), xw)
-        def ywin(yrel, w, r):
-            yb = bc(yrel, r, W)
-            yw = jnp.where(yb == ycon[0], bc(w[6], r, W), zero)
-            yw = jnp.where(yb == ycon[1], bc(w[7], r, W), yw)
-            return jnp.where(yb == ycon[2], bc(w[8], r, W), yw)
-        def sides(yrel, u, car, w, zn, r):
-            xw = xwin(u, w, r)
-            yw = ywin(yrel, w, r)
-            if variant == 0:
-                left = jnp.concatenate([bc(car[f] * zn[z], r, 16) * xw for f in range(4) for z in range(4)], 0)
-                return left, yw
-            left = jnp.concatenate([bc(zn[z], r, 16) * xw for z in range(4)], 0)
-            right = jnp.concatenate([bc(car[f], r, W) * yw for f in range(4)], 0)
-            return left, right
-        def product(yrel, data, j):
-            l0, r0 = sides(yrel, *data, 2 * j)
-            l1, r1 = sides(yrel, *data, 2 * j + 1)
-            left = jnp.concatenate([l0, l1], 1)
-            right = jnp.concatenate([r0, r1], 1)
-            return lax.dot_general(right, left, (((1,), (1,)), ((), ())), preferred_element_type=F32)
-        def add(base, res):
-            rows = pl.ds(pl.multiple_of(base, 8), W)
-            if variant == 0:
-                acc[rows, :] += res
-            else:
-                for f in range(4):
-                    acc[f, rows, 0:64] += res[f * W:(f + 1) * W]
-        def group(g, carry):
-            bases, more, yrel = scan(g) if not pre else carry
-            data = prep(g)
-            nxt = scan(jnp.minimum(g + 1, ROWS // 8 - 1)) if pre else 0
-            res = [product(yrel, data, j) for j in range(4)]
-            for j in range(4):
-                add(bases[j], res[j])
-            @pl.when(more)
+        left_n = n - c * UNIT
+        rr = pl.ds(pl.multiple_of(b * ROWS + jnp.minimum(c, ROWS // UR - 1) * UR, UR), UR)
+        cl = cells[rr, :]
+        live = place_id < left_n
+        m = jnp.where(live, mass[rr, :], 0.0)
+        y = cl & 127
+        first = jnp.broadcast_to(y[:, 0:1], (UR, 128)) & ~7
+        up = jnp.concatenate([first[0:1]] + [first[i - 1:i] for i in range(1, UR)], 0)
+        first = jnp.where(odd, up, first)
+        yrel = y - first
+        spread = jnp.where(live, yrel, 0)
+        bases = [first[2*j, 0] for j in range(UR // 2)]
+        u = ((cl >> 7) & 7).astype(F32)
+        top = cl >= 1024
+        car = [m] + [m * vel[k, rr, :] for k in range(3)]
+        w = [wt[r, rr, :] for r in range(9)]
+        zn = [jnp.where(top, 0.0, w[0]), jnp.where(top, w[0], w[1]),
+              jnp.where(top, w[1], w[2]), jnp.where(top, w[2], 0.0)]
+        return bases, spread, yrel.astype(F32), (u, car, zn, w)
+
+    def sides(yrel, data, r):
+        u, car, zn, w = data
+        ub = bc(u, r, 16)
+        xw = jnp.where(ub == xcon[0], bc(w[3], r, 16), zero)
+        xw = jnp.where(ub == xcon[1], bc(w[4], r, 16), xw)
+        xw = jnp.where(ub == xcon[2], bc(w[5], r, 16), xw)
+        yb = bc(yrel, r, W)
+        yw = jnp.where(yb == ycon[0], bc(w[6], r, W), zero)
+        yw = jnp.where(yb == ycon[1], bc(w[7], r, W), yw)
+        yw = jnp.where(yb == ycon[2], bc(w[8], r, W), yw)
+        return [bc(zn[z], r, 16) * xw for z in range(4)], [bc(car[f], r, W) * yw for f in range(4)]
+    def build(yrel, data, j, i):
+        for k in range(2):
+            ls, rs = sides(yrel, data, 2 * j + k)
+            for z in range(4):
+                lbuf[i, z * 16:(z + 1) * 16, k * 128:(k + 1) * 128] = ls[z]
+            for f in range(4):
+                rbuf[i, f * W:(f + 1) * W, k * 128:(k + 1) * 128] = rs[f]
+    def multiply(i):
+        left = lbuf[i]
+        left = jnp.concatenate([left, left], 0)
+        res = lax.dot_general(rbuf[i], left, (((1,), (1,)), ((), ())), preferred_element_type=F32)
+        for h in range(2):
+            prod[i, h] = jnp.where(lane_lo, res[2 * h * W:(2 * h + 1) * W], res[(2 * h + 1) * W:(2 * h + 2) * W])
+    def accumulate(i, b, base):
+        rows = pl.ds(pl.multiple_of(base, 8), W)
+        for h in range(2):
+            acc[b, h, rows, :] += prod[i, h]
+
+    def units(b):
+        return (counts[b] + (UNIT - 1)) // UNIT
+
+    def part(q, pend):
+        for c in copies(q):
+            c.wait()
+        last = q * PB + PB - 1
+        total = lax.fori_loop(q * PB, q * PB + PB, lambda b, t: t + units(b), 0)
+        def group(g, state):
+            b, c, (older, old) = state
+            for i in range(NCH):
+                accumulate(i, *older[i])
+            for i in range(NCH):
+                multiply(i)
+            new = []
+            far = None
+            items = []
+            i = 0
+            for _ in range(U):
+                bases, spread, yrel, data = load(b, c)
+                items.append((b, c))
+                for j in range(UR // 2):
+                    build(yrel, data, j, i)
+                    new.append((b, bases[j]))
+                    i += 1
+                far = spread if far is None else jnp.maximum(far, spread)
+                done = jnp.logical_and(c + 1 >= units(b), b < last)
+                b, c = jnp.where(done, b + 1, b), jnp.where(done, 0, c + 1)
+            @pl.when(jnp.max(far) >= 24)
             def _():
-                def window(off, _):
-                    shift = (off * W).astype(F32)
-                    for j in range(4):
-                        base = bases[j] + off * W
-                        @pl.when(base < 130)
-                        def _():
-                            add(base, product(yrel - shift, data, j))
-                    return 0
-                lax.fori_loop(1, 5, window, 0)
-            return nxt
-        if skip != 1:
-            lax.fori_loop(0, (n + 1023) // 1024, group, scan(0) if pre else 0)
-        up = lax.rem(b + 1, BLOCKS); dn = lax.rem(b + BLOCKS - 1, BLOCKS)
-        def place(f, z, own, halo):
-            out[f, z, pl.ds(pl.multiple_of(b * 8, 8), 8), :] += own
-            out[f, z, pl.ds(pl.multiple_of(up * 8, 8), 8), :] += jnp.where(sub == 0, halo, 0.0)
-            out[f, z, pl.ds(pl.multiple_of(dn * 8, 8), 8), :] += jnp.where(sub == 7, halo, 0.0)
-        if skip == 2:
-            return 0
-        if variant == 0:
-            acc[128:129] += acc[0:1]
-            acc[1:2] += acc[129:130]
-            t = acc[1:129, :].T
-            for f in range(4):
-                for z in range(4):
-                    o = (f * 4 + z) * 16
-                    place(f, z, t[o:o+8], t[o+8:o+16])
-        else:
-            for f in range(4):
-                acc[f, 128:129] += acc[f, 0:1]
-                acc[f, 1:2] += acc[f, 129:130]
-                t = acc[f, 1:129, :].T
-                for z in range(4):
-                    o = z * 16
-                    place(f, z, t[o:o+8], t[o+8:o+16])
-        return 0
-    lax.fori_loop(0, BPS, block, 0)
+                def one(bb, cc):
+                    bases, spread, yrel, data = load(bb, cc)
+                    for j in range(UR // 2):
+                        def window(off, _):
+                            base = bases[j] + off * W
+                            @pl.when(base < 130)
+                            def _():
+                                build(yrel - (off * W).astype(F32), data, j, NCH)
+                                multiply(NCH)
+                                accumulate(NCH, bb, base)
+                            return 0
+                        lax.fori_loop(1, 5, window, 0)
+                for bb, cc in items:
+                    one(bb, cc)
+            return b, c, (old, tuple(new))
+        _, _, pend = lax.fori_loop(0, (total + U - 1) // U, group, (q * PB, 0, pend))
+        return pend
+    if skip != 1:
+        none = tuple((0, 0) for _ in range(NCH))
+        older, old = lax.fori_loop(0, PARTS, part, (none, none))
+        for i in range(NCH):
+            accumulate(i, *older[i])
+        for i in range(NCH):
+            multiply(i)
+        for i in range(NCH):
+            accumulate(i, *old[i])
+    else:
+        for q in range(PARTS):
+            for c in copies(q):
+                c.wait()
+
+    def finish(b0, _):
+        for k in range(UF):
+            b = b0 * UF + k
+            for h in range(2):
+                head = acc[b, h, 1:9] + jnp.where(sub == 0, acc[b, h, 129:137], 0.0)
+                tail = acc[b, h, 121:129] + jnp.where(sub == 7, jnp.broadcast_to(acc[b, h, 0:1], (8, 128)), 0.0)
+                tbuf[b, h] = jnp.concatenate([head, acc[b, h, 9:121], tail], 0).T
+        return 0
+    if skip != 2:
+        lax.fori_loop(0, BLOCKS // UF, finish, 0)
+    def seams(b, _):
+        here = pl.ds(pl.multiple_of(b * 8, 8), 8)
+        dn = (b + BLOCKS - 1) & (BLOCKS - 1)
+        up = (b + 1) & (BLOCKS - 1)
+        for f in range(4):
+            for z in range(4):
+                o = (f % 2) * 64 + z * 16
+                out[f, z, here, :] = (tbuf[b, f // 2, o:o + 8]
+                    + jnp.where(sub == 0, tbuf[dn, f // 2, o + 8:o + 16], 0.0)
+                    + jnp.where(sub == 7, tbuf[up, f // 2, o + 8:o + 16], 0.0))
+        return 0
+    if skip != 3:
+        lax.fori_loop(0, BLOCKS, seams, 0)
 
 def deposit(cfg, counts, mass, vel, wt, cells):
-    variant = cfg[0]
-    R = BPS * ROWS
-    accs = pltpu.VMEM((160, 256), F32) if variant == 0 else pltpu.VMEM((4, 160, 128), F32)
+    UR, U, PARTS, skip, UF = cfg
+    NCH = UR * U // 2
+    hbm = pl.BlockSpec(memory_space=pltpu.MemorySpace.HBM)
     return pl.pallas_call(
         functools.partial(dep_kernel, cfg),
-        grid=(BLOCKS // BPS,),
-        in_specs=[pl.BlockSpec(memory_space=pltpu.SMEM),
-                  pl.BlockSpec((R, 128), lambda i: (i, 0)),
-                  pl.BlockSpec((3, R, 128), lambda i: (0, i, 0)),
-                  pl.BlockSpec((9, R, 128), lambda i: (0, i, 0)),
-                  pl.BlockSpec((R, 128), lambda i: (i, 0))],
-        out_specs=pl.BlockSpec((4, 4, 256, 128), lambda i: (0, 0, 0, 0)),
+        in_specs=[pl.BlockSpec(memory_space=pltpu.SMEM), hbm, hbm, hbm, hbm],
+        out_specs=pl.BlockSpec(memory_space=pltpu.VMEM),
         out_shape=jax.ShapeDtypeStruct((4, 4, 256, 128), F32),
-        scratch_shapes=[accs],
-        compiler_params=pltpu.CompilerParams(vmem_limit_bytes=50 << 20),
+        scratch_shapes=[pltpu.VMEM((1024, 128), F32), pltpu.VMEM((3, 1024, 128), F32), pltpu.VMEM((9, 1024, 128), F32),
+                        pltpu.VMEM((1024, 128), jnp.int32), pltpu.VMEM((32, 2, 160, 128), F32),
+                        pltpu.VMEM((32, 2, 128, 128), F32),
+                        pltpu.VMEM((NCH + 1, 64, 256), BF), pltpu.VMEM((NCH + 1, 4 * W, 256), BF), pltpu.VMEM((NCH + 1, 2, W, 128), F32),
+                        pltpu.SemaphoreType.DMA((4, PARTS))],
+        compiler_params=pltpu.CompilerParams(vmem_limit_bytes=60 << 20),
     )(counts, mass.reshape(1024, 128), vel.reshape(3, 1024, 128), wt.reshape(9, 1024, 128), cells.reshape(1024, 128))
 
 MASS_FLOOR = 0.2
@@ -344,7 +393,7 @@
 
 
 def per_device(particle_mass, particle_velocity, spline_weights, particle_cells, block_counts, friction, contact_flags):
-    dep = deposit((1, 0, 0), block_counts.reshape(32), particle_mass, particle_velocity, spline_weights, particle_cells)
+    dep = deposit((4, 8, 2, 0, 4), block_counts.reshape(32), particle_mass, particle_velocity, spline_weights, particle_cells)
     return exchange(friction, dep, contact_flags)
 
 

time: 82.7 us -> 60.4 us (0.73)
  the two profiles are of different devices: /device:TPU:1 before, /device:TPU:136 now
where the time goes in v1:
time: 60.4 us; the launch traced here: 60.3 us
  Pallas kernels  57.1 us (95%)
  local copies, waits for them, and re-layouts  2.47 us (4%)
  between operations  0.69 us (1%)
    pallas_call x1, Pallas kernels, exchange(): pl.pallas_call(comm_kernel, in_specs=[pl.BlockSpec(memory_space=pltpu.SME...  33.7 us
    pallas_call x1, Pallas kernels, deposit(): pl.pallas_call(functools.partial(dep_kernel, cfg), in_specs=[pl.BlockSpec...  23.5 us
    unnamed x5, local copies, waits for them, and re-layouts  2.47 us

profile of v1, /device:TPU:136, one launch (start us, length us, event | category | flops | bytes accessed | tf_op | source)
XLA Modules:
  0.0 60.3 jit_solution(16793624720623824847)
XLA Ops:
  0.7 0.0 copy-start.1
  0.7 23.5 %shard_map.73.dep = f32[4,4,256,128]{3,2,1,0:T(8,128)} custom-call(s32[32]{0:T(128)} %bitcast.9, f32[1024,128]{1,0:T(8,128)} %bitcast.7, f32[3,1024,128]{2,1,0:T(8,128)} %bitcast.6, f32[9,1024,128]{2,1,0:T(8,128)} %bitcast.5, s32[1024,128]{1,0:T(8,128)} %bitcast.8), custom_call_target="tpu_custom_call" | custom-call | tf_op jit(solution)/shard_map/pallas_call | solution.py:191
  24.1 0.0 copy-done.1
  24.2 0.0 copy-start
  24.2 1.6 %copy-done = f32[4,4,256,128]{3,2,1,0:T(8,128)S(1)} copy-done((f32[4,4,256,128]{3,2,1,0:T(8,128)S(1)}, f32[4,4,256,128]{3,2,1,0:T(8,128)}, u32[]{:S(2)}) %copy-start) | copy-done | bytes 2097176
  25.7 33.7 %shard_map.74 = f32[1,3,2,256,128]{4,3,2,1,0:T(8,128)S(1)} custom-call(f32[1]{0:T(128)S(6)} %copy.9.fric, f32[4,4,256,128]{3,2,1,0:T(8,128)S(1)} %copy-done, s32[2,256,128]{2,1,0:T(8,128)S(1)} %copy-done.1), custom_call_target="tpu_custom_call" | custom-call | tf_op jit(solution)/shard_map/pallas_call | solution.py:378
  59.4 0.9 %copy.10 = f32[1,3,2,256,128]{4,3,2,1,0:T(8,128)} copy(f32[1,3,2,256,128]{4,3,2,1,0:T(8,128)S(1)} %shard_map.74) | data formatting | bytes 1572864
Async XLA Ops:
  0.7 23.5 %copy-start.1 = (s32[2,256,128]{2,1,0:T(8,128)S(1)}, s32[2,256,128]{2,1,0:T(8,128)}, u32[]{:S(2)}) copy-start(s32[2,256,128]{2,1,0:T(8,128)} %flags.1) | copy-start | bytes 786436
  24.2 1.6 %copy-start = (f32[4,4,256,128]{3,2,1,0:T(8,128)S(1)}, f32[4,4,256,128]{3,2,1,0:T(8,128)}, u32[]{:S(2)}) copy-start(f32[4,4,256,128]{3,2,1,0:T(8,128)} %shard_map.73.dep) | copy-start | bytes 6291460

commit v2 on v1

--- a/solution.py
+++ b/solution.py
@@ -13,19 +13,18 @@
     r = lax.broadcasted_iota(jnp.int32, (n, k), 0)
     return fn(r).astype(F32).astype(BF)
 
-def dep_kernel(cfg, counts, mass_h, vel_h, wt_h, cells_h, out, mass, vel, wt, cells, acc, tbuf, lbuf, rbuf, prod, sems):
-    UR, U, PARTS, skip, UF = cfg
+def dep_kernel(cfg, counts, mass_h, vel_h, wt_h, cells_h, out, mass, vel, wt, cells, acc, tbuf, lbuf, rbuf, prod, sems, obuf, osem):
+    UR, U, HEAD, skip, UF, MODE = cfg
     UNIT = UR * 128
     NCH = UR * U // 2
-    PB = BLOCKS // PARTS
-    PR = PB * ROWS
+    spans = [(0, HEAD), (HEAD, BLOCKS)]
     def copies(q):
-        r = pl.ds(q * PR, PR)
+        r = pl.ds(spans[q][0] * ROWS, (spans[q][1] - spans[q][0]) * ROWS)
         return [pltpu.make_async_copy(mass_h.at[r], mass.at[r], sems.at[0, q]),
                 pltpu.make_async_copy(vel_h.at[:, r], vel.at[:, r], sems.at[1, q]),
                 pltpu.make_async_copy(wt_h.at[:, r], wt.at[:, r], sems.at[2, q]),
                 pltpu.make_async_copy(cells_h.at[r], cells.at[r], sems.at[3, q])]
-    for q in range(PARTS):
+    for q in range(2):
         for c in copies(q):
             c.start()
     ycon = [rows_const(W, lambda r, t=t: r - t, 128) for t in range(3)]
@@ -88,12 +87,16 @@
                 lbuf[i, z * 16:(z + 1) * 16, k * 128:(k + 1) * 128] = ls[z]
             for f in range(4):
                 rbuf[i, f * W:(f + 1) * W, k * 128:(k + 1) * 128] = rs[f]
-    def multiply(i):
+    def multiply(i, where=None):
         left = lbuf[i]
         left = jnp.concatenate([left, left], 0)
         res = lax.dot_general(rbuf[i], left, (((1,), (1,)), ((), ())), preferred_element_type=F32)
         for h in range(2):
-            prod[i, h] = jnp.where(lane_lo, res[2 * h * W:(2 * h + 1) * W], res[(2 * h + 1) * W:(2 * h + 2) * W])
+            both = jnp.where(lane_lo, res[2 * h * W:(2 * h + 1) * W], res[(2 * h + 1) * W:(2 * h + 2) * W])
+            if where is None:
+                prod[i, h] = both
+            else:
+                acc[where[0], h, pl.ds(pl.multiple_of(where[1], 8), W), :] += both
     def accumulate(i, b, base):
         rows = pl.ds(pl.multiple_of(base, 8), W)
         for h in range(2):
@@ -103,21 +106,37 @@
         return (counts[b] + (UNIT - 1)) // UNIT
 
     def part(q, pend):
-        for c in copies(q):
-            c.wait()
-        last = q * PB + PB - 1
-        total = lax.fori_loop(q * PB, q * PB + PB, lambda b, t: t + units(b), 0)
+        first_block = jnp.where(q == 0, 0, HEAD)
+        last = jnp.where(q == 0, HEAD, BLOCKS) - 1
+        @pl.when(q == 0)
+        def _():
+            for c in copies(0):
+                c.wait()
+        @pl.when(q == 1)
+        def _():
+            for c in copies(1):
+                c.wait()
+        total = lax.fori_loop(first_block, last + 1, lambda b, t: t + units(b), 0)
         def group(g, state):
             b, c, (older, old) = state
-            for i in range(NCH):
-                accumulate(i, *older[i])
-            for i in range(NCH):
-                multiply(i)
             new = []
             far = None
             items = []
             i = 0
+            if MODE == 0:
+                for i in range(NCH):
+                    accumulate(i, *older[i])
+                for i in range(NCH):
+                    multiply(i)
+            i = 0
             for _ in range(U):
+                if MODE == 1:
+                    for j in range(UR // 2):
+                        accumulate(i + j, *older[i + j])
+                        multiply(i + j)
+                if MODE == 2:
+                    for j in range(UR // 2):
+                        multiply(i + j, old[i + j])
                 bases, spread, yrel, data = load(b, c)
                 items.append((b, c))
                 for j in range(UR // 2):
@@ -144,19 +163,23 @@
                 for bb, cc in items:
                     one(bb, cc)
             return b, c, (old, tuple(new))
-        _, _, pend = lax.fori_loop(0, (total + U - 1) // U, group, (q * PB, 0, pend))
+        _, _, pend = lax.fori_loop(0, (total + U - 1) // U, group, (first_block, 0, pend))
         return pend
     if skip != 1:
         none = tuple((0, 0) for _ in range(NCH))
-        older, old = lax.fori_loop(0, PARTS, part, (none, none))
-        for i in range(NCH):
-            accumulate(i, *older[i])
-        for i in range(NCH):
-            multiply(i)
-        for i in range(NCH):
-            accumulate(i, *old[i])
+        older, old = lax.fori_loop(0, 2, part, (none, none))
+        if MODE == 2:
+            for i in range(NCH):
+                multiply(i, old[i])
+        else:
+            for i in range(NCH):
+                accumulate(i, *older[i])
+            for i in range(NCH):
+                multiply(i)
+            for i in range(NCH):
+                accumulate(i, *old[i])
     else:
-        for q in range(PARTS):
+        for q in range(2):
             for c in copies(q):
                 c.wait()
 
@@ -170,34 +193,42 @@
         return 0
     if skip != 2:
         lax.fori_loop(0, BLOCKS // UF, finish, 0)
-    def seams(b, _):
-        here = pl.ds(pl.multiple_of(b * 8, 8), 8)
-        dn = (b + BLOCKS - 1) & (BLOCKS - 1)
-        up = (b + 1) & (BLOCKS - 1)
-        for f in range(4):
-            for z in range(4):
-                o = (f % 2) * 64 + z * 16
-                out[f, z, here, :] = (tbuf[b, f // 2, o:o + 8]
-                    + jnp.where(sub == 0, tbuf[dn, f // 2, o + 8:o + 16], 0.0)
-                    + jnp.where(sub == 7, tbuf[up, f // 2, o + 8:o + 16], 0.0))
+    def piece(p):
+        return pltpu.make_async_copy(obuf.at[p], out.at[p], osem.at[p])
+    def seams(p, _):
+        for j in range(4):
+            b = p * 4 + j
+            dn = (b + BLOCKS - 1) & (BLOCKS - 1)
+            up = (b + 1) & (BLOCKS - 1)
+            for k in range(16):
+                o = (k // 4 % 2) * 64 + k % 4 * 16
+                h = k // 8
+                obuf[p, k, 8 * j:8 * j + 8, :] = (tbuf[b, h, o:o + 8]
+                    + jnp.where(sub == 0, tbuf[dn, h, o + 8:o + 16], 0.0)
+                    + jnp.where(sub == 7, tbuf[up, h, o + 8:o + 16], 0.0))
+        piece(p).start()
         return 0
     if skip != 3:
-        lax.fori_loop(0, BLOCKS, seams, 0)
+        lax.fori_loop(0, 8, seams, 0)
+        def drain(p, _):
+            piece(p).wait()
+            return 0
+        lax.fori_loop(0, 8, drain, 0)
 
 def deposit(cfg, counts, mass, vel, wt, cells):
-    UR, U, PARTS, skip, UF = cfg
+    UR, U, HEAD, skip, UF, MODE = cfg
     NCH = UR * U // 2
     hbm = pl.BlockSpec(memory_space=pltpu.MemorySpace.HBM)
     return pl.pallas_call(
         functools.partial(dep_kernel, cfg),
         in_specs=[pl.BlockSpec(memory_space=pltpu.SMEM), hbm, hbm, hbm, hbm],
-        out_specs=pl.BlockSpec(memory_space=pltpu.VMEM),
-        out_shape=jax.ShapeDtypeStruct((4, 4, 256, 128), F32),
+        out_specs=hbm,
+        out_shape=jax.ShapeDtypeStruct((8, 16, 32, 128), F32),
         scratch_shapes=[pltpu.VMEM((1024, 128), F32), pltpu.VMEM((3, 1024, 128), F32), pltpu.VMEM((9, 1024, 128), F32),
                         pltpu.VMEM((1024, 128), jnp.int32), pltpu.VMEM((32, 2, 160, 128), F32),
                         pltpu.VMEM((32, 2, 128, 128), F32),
                         pltpu.VMEM((NCH + 1, 64, 256), BF), pltpu.VMEM((NCH + 1, 4 * W, 256), BF), pltpu.VMEM((NCH + 1, 2, W, 128), F32),
-                        pltpu.SemaphoreType.DMA((4, PARTS))],
+                        pltpu.SemaphoreType.DMA((4, 2)), pltpu.VMEM((8, 16, 32, 128), F32), pltpu.SemaphoreType.DMA((8,))],
         compiler_params=pltpu.CompilerParams(vmem_limit_bytes=60 << 20),
     )(counts, mass.reshape(1024, 128), vel.reshape(3, 1024, 128), wt.reshape(9, 1024, 128), cells.reshape(1024, 128))
 
@@ -209,7 +240,7 @@
 MESH = pl.DeviceIdType.MESH
 
 
-def comm_kernel(fric, dep, flags, out, hsend, hrecv, nf, mass, gradz, rsend, rrecv, cbuf,
+def comm_kernel(fric, dep_h, flags_h, out, dep, flags, obuf, d_s, f_s, o_s, hsend, hrecv, nf, mass, gradz, rsend, rrecv, cbuf,
                 h_ss, h_rs, r_ss, r_rs, c_ss, c_rs):
     slabs = lax.axis_size("gz")
     g = lax.axis_index("gz")
@@ -219,6 +250,17 @@
     s_lo = jnp.where(g == 0, 0.0, 1.0)
     s_hi = jnp.where(g == slabs - 1, 0.0, 1.0)
 
+    def fetch(p):
+        return pltpu.make_async_copy(dep_h.at[p], dep.at[p], d_s.at[p])
+
+    def start_fetch(k, _):
+        fetch(lax.rem(me + 1 + k, PIECES)).start()
+        return 0
+
+    lax.fori_loop(0, PIECES, start_fetch, 0)
+    fetch_flags = pltpu.make_async_copy(flags_h, flags, f_s)
+    fetch_flags.start()
+
     barrier = pltpu.get_barrier_semaphore()
     for other in (lo, hi):
         pl.semaphore_signal(barrier, inc=1, device_id={"gz": other, "mat": me}, device_id_type=MESH)
@@ -257,12 +299,12 @@
 
     def pack(k, _):
         p = lax.rem(me + 1 + k, PIECES)
-        x = cols(p)
+        fetch(p).wait()
         for f in range(4):
-            hsend[0, p, f] = dep[f, 0, x, :].astype(jnp.bfloat16)
-            hsend[1, p, f] = dep[f, 3, x, :].astype(jnp.bfloat16)
-        hsend[0, p, 4] = dep[0, 1, x, :].astype(jnp.bfloat16)
-        hsend[1, p, 4] = dep[0, 2, x, :].astype(jnp.bfloat16)
+            hsend[0, p, f] = dep[p, 4 * f + 0].astype(jnp.bfloat16)
+            hsend[1, p, f] = dep[p, 4 * f + 3].astype(jnp.bfloat16)
+        hsend[0, p, 4] = dep[p, 1].astype(jnp.bfloat16)
+        hsend[1, p, 4] = dep[p, 2].astype(jnp.bfloat16)
         return 0
 
     lax.fori_loop(0, PIECES, pack, 0)
@@ -281,8 +323,8 @@
         halo(1, p).wait_recv()
         x = cols(p)
         for f in range(4):
-            low = dep[f, 1, x, :] + s_lo * hrecv[1, p, f].astype(jnp.float32)
-            high = dep[f, 2, x, :] + s_hi * hrecv[0, p, f].astype(jnp.float32)
+            low = dep[p, 4 * f + 1] + s_lo * hrecv[1, p, f].astype(jnp.float32)
+            high = dep[p, 4 * f + 2] + s_hi * hrecv[0, p, f].astype(jnp.float32)
             nf[f, 0, x, :] = low
             nf[f, 1, x, :] = high
             rsend[p, f, 0] = low.astype(jnp.bfloat16)
@@ -291,8 +333,8 @@
                 xm = pl.ds(pl.multiple_of(p * COLS + 8, 8), COLS)
                 mass[0, xm, :] = low
                 mass[1, xm, :] = high
-                below = s_lo * (hrecv[1, p, 4].astype(jnp.float32) + dep[0, 0, x, :])
-                above = s_hi * (hrecv[0, p, 4].astype(jnp.float32) + dep[0, 3, x, :])
+                below = s_lo * (hrecv[1, p, 4].astype(jnp.float32) + dep[p, 0])
+                above = s_hi * (hrecv[0, p, 4].astype(jnp.float32) + dep[p, 3])
                 gradz[0, x, :] = (high - below) * 0.5
                 gradz[1, x, :] = (above - low) * 0.5
 
@@ -322,6 +364,10 @@
 
     lax.fori_loop(0, PIECES - 1, start_spread, 0)
     friction = fric[0]
+    fetch_flags.wait()
+
+    def result(p):
+        return pltpu.make_async_copy(obuf.at[:, :, cols(p)], out.at[0, :, :, cols(p)], o_s.at[p])
 
     def finish(p):
         for z in range(2):
@@ -343,14 +389,16 @@
             factor = jnp.minimum(friction * approach, slip) / jnp.maximum(slip, SLIP_FLOOR)
             flag = flags[z, x, :].astype(jnp.float32)
             for d in range(3):
-                out[0, d, z, x, :] = speed[d] - flag * (approach * normal[d] + factor * tangent[d])
+                obuf[d, z, x, :] = speed[d] - flag * (approach * normal[d] + factor * tangent[d])
 
     finish(me)
+    result(me).start()
 
     def finish_step(k, _):
         p = lax.rem(me + PIECES - 1 - k, PIECES)
         spreaded(p).wait_recv()
         finish(p)
+        result(p).start()
         return 0
 
     lax.fori_loop(0, PIECES - 1, finish_step, 0)
@@ -366,21 +414,24 @@
     def drain_halo(p, _):
         halo(0, p).wait_send()
         halo(1, p).wait_send()
+        result(p).wait()
         return 0
 
     lax.fori_loop(0, PIECES, drain_halo, 0)
 
 
 def exchange(friction, dep, flags):
-    vm = pl.BlockSpec(memory_space=pltpu.VMEM)
+    hbm = pl.BlockSpec(memory_space=pltpu.MemorySpace.HBM)
     f32, bf = jnp.float32, jnp.bfloat16
     dma = pltpu.SemaphoreType.DMA
     return pl.pallas_call(
         comm_kernel,
-        in_specs=[pl.BlockSpec(memory_space=pltpu.SMEM), vm, vm],
-        out_specs=vm,
+        in_specs=[pl.BlockSpec(memory_space=pltpu.SMEM), hbm, hbm],
+        out_specs=hbm,
         out_shape=jax.ShapeDtypeStruct((1, 3, 2, 256, 128), f32),
         scratch_shapes=[
+            pltpu.VMEM((PIECES, 16, COLS, 128), f32), pltpu.VMEM((2, 256, 128), jnp.int32),
+            pltpu.VMEM((3, 2, 256, 128), f32), dma((PIECES,)), dma, dma((PIECES,)),
             pltpu.VMEM((2, PIECES, 5, COLS, 128), bf), pltpu.VMEM((2, PIECES, 5, COLS, 128), bf),
             pltpu.VMEM((4, 2, 256, 128), f32), pltpu.VMEM((2, 272, 128), f32),
             pltpu.VMEM((2, 256, 128), f32),
@@ -388,12 +439,12 @@
             pltpu.VMEM((PIECES, 3, 2, COLS, 128), bf),
             dma((2, PIECES)), dma((2, PIECES)), dma((PIECES,)), dma((PIECES,)), dma((PIECES,)), dma((PIECES,)),
         ],
-        compiler_params=pltpu.CompilerParams(collective_id=0, has_side_effects=True, vmem_limit_bytes=40 << 20),
+        compiler_params=pltpu.CompilerParams(collective_id=0, has_side_effects=True, vmem_limit_bytes=60 << 20),
     )(friction, dep, flags)
 
 
 def per_device(particle_mass, particle_velocity, spline_weights, particle_cells, block_counts, friction, contact_flags):
-    dep = deposit((4, 8, 2, 0, 4), block_counts.reshape(32), particle_mass, particle_velocity, spline_weights, particle_cells)
+    dep = deposit((4, 8, 4, 0, 4, 2), block_counts.reshape(32), particle_mass, particle_velocity, spline_weights, particle_cells)
     return exchange(friction, dep, contact_flags)
 
 

time: 60.4 us -> 58.4 us (0.967)
  the two profiles are of different devices: /device:TPU:136 before, /device:TPU:40 now
where the time goes in v2:
time: 58.4 us; the launch traced here: 58.2 us
  Pallas kernels  55.5 us (95%)
  local copies, waits for them, and re-layouts  2.06 us (4%)
  between operations  0.67 us (1%)
    pallas_call x1, Pallas kernels, exchange(): pl.pallas_call(comm_kernel, in_specs=[pl.BlockSpec(memory_space=pltpu.SME...  36.1 us
    pallas_call x1, Pallas kernels, deposit(): pl.pallas_call(functools.partial(dep_kernel, cfg), in_specs=[pl.BlockSpec...  19.4 us
    unnamed x1, local copies, waits for them, and re-layouts  2.06 us

profile of v2, /device:TPU:40, one launch (start us, length us, event | category | flops | bytes accessed | tf_op | source)
XLA Modules:
  0.0 58.2 jit_solution(16140071345054805925)
XLA Ops:
  0.7 19.4 %shard_map.73.dep_h = f32[8,16,32,128]{3,2,1,0:T(8,128)} custom-call(s32[32]{0:T(128)} %bitcast.9, f32[1024,128]{1,0:T(8,128)} %bitcast.7, f32[3,1024,128]{2,1,0:T(8,128)} %bitcast.6, f32[9,1024,128]{2,1,0:T(8,128)} %bitcast.5, s32[1024,128]{1,0:T(8,128)} %bitcast.8), custom_call_target="tpu_custom_call" | custom-call | tf_op jit(solution)/shard_map/pallas_call | solution.py:222
  20.1 36.1 %shard_map.74 = f32[1,3,2,256,128]{4,3,2,1,0:T(8,128)} custom-call(f32[1]{0:T(128)S(6)} %copy.9.fric, f32[8,16,32,128]{3,2,1,0:T(8,128)} %shard_map.73.dep_h, s32[2,256,128]{2,1,0:T(8,128)} %flags_h.1), custom_call_target="tpu_custom_call" | custom-call | tf_op jit(solution)/shard_map/pallas_call | solution.py:427
  56.2 2.1 %copy.10 = f32[1,3,2,256,128]{4,3,2,1,0:T(8,128)} copy(f32[1,3,2,256,128]{4,3,2,1,0:T(8,128)} %shard_map.74) | data formatting | bytes 1572864

commit v3 on v2

v3 whole, which is shorter than its diff:
```python
import functools
import jax
import jax.numpy as jnp
from jax import lax
from jax.experimental import pallas as pl
from jax.experimental.pallas import tpu as pltpu
from jax.sharding import PartitionSpec as P

BLOCKS = 32
SLOTS = 4096
ROWS = SLOTS // 128
UR = 4
UNIT = UR * 128
PER_BLOCK = SLOTS // UNIT
W = 24
HEAD = 4
F32, BF = jnp.float32, jnp.bfloat16


def deposit_kernel(U, XP, ORDER, counts, mass_h, vel_h, wt_h, cells_h, out, mass, vel, wt, cells, acc, tbuf, prep,
                   lbuf, rbuf, obuf, urow, uleft, ubase, in_sem, out_sem):
    chunks = U * UR // 2

    def copies(q):
        first, count = ((0, HEAD), (HEAD, BLOCKS - HEAD))[q]
        r = pl.ds(first * ROWS, count * ROWS)
        return [pltpu.make_async_copy(mass_h.at[r], mass.at[r], in_sem.at[0, q]),
                pltpu.make_async_copy(vel_h.at[:, r], vel.at[:, r], in_sem.at[1, q]),
                pltpu.make_async_copy(wt_h.at[:, r], wt.at[:, r], in_sem.at[2, q]),
                pltpu.make_async_copy(cells_h.at[r], cells.at[r], in_sem.at[3, q])]

    for q in range(2):
        for c in copies(q):
            c.start()

    sub = lax.broadcasted_iota(jnp.int32, (8, 128), 0)
    usub = lax.broadcasted_iota(jnp.int32, (UR, 128), 0)
    place_id = usub * 128 + lax.broadcasted_iota(jnp.int32, (UR, 128), 1)
    odd = (usub & 1) == 1
    row16 = lax.broadcasted_iota(jnp.int32, (16, 128), 0)

    def const(values):
        return values.astype(F32).astype(BF)

    xcon = [const((row16 - p + 1) & 15) for p in range(3)]
    ycon = [const(row16 - t) for t in range(3)]
    ycon_b = [const(16 + (row16 & 7) - t) for t in range(3)]
    upper = const(row16) < jnp.asarray(8, BF)
    zero = jnp.zeros((), BF)

    def dead(i, row):
        urow[i] = row
        uleft[i] = 0

    for i in range(2 * U):
        dead(i, 0)
    for i in range(2 * chunks):
        ubase[i] = 0

    def list_block(b, at):
        n = counts[b]
        for c in range(PER_BLOCK):
            urow[at + c] = b * ROWS + c * UR
            uleft[at + c] = n - c * UNIT
        return at + (n + (UNIT - 1)) // UNIT

    head_end = lax.fori_loop(0, HEAD, list_block, 2 * U)
    end = lax.fori_loop(HEAD, BLOCKS, list_block, head_end)
    for i in range(3 * U):
        dead(end + i, BLOCKS * ROWS - UR)

    def clear(b, _):
        acc[b] = jnp.zeros(acc.shape[1:], F32)
        return 0

    lax.fori_loop(0, BLOCKS, clear, 0)
    prep[...] = jnp.zeros(prep.shape, F32)
    lbuf[...] = jnp.zeros(lbuf.shape, BF)
    rbuf[...] = jnp.zeros(rbuf.shape, BF)

    def prepare(slot, unit):
        row = urow[unit]
        rr = pl.ds(pl.multiple_of(row, UR), UR)
        cl = cells[rr, :]
        live = place_id < uleft[unit]
        m = jnp.where(live, mass[rr, :], 0.0)
        y = cl & 127
        first = jnp.broadcast_to(y[:, 0:1], (UR, 128)) & ~7
        before = jnp.concatenate([first[0:1]] + [first[i - 1:i] for i in range(1, UR)], 0)
        first = jnp.where(odd, before, first)
        yrel = y - first
        top = cl >= 1024
        w = [wt[a, rr, :] for a in range(3)]
        prep[slot, 0] = yrel.astype(F32)
        prep[slot, 1] = ((cl >> 7) & 7).astype(F32)
        prep[slot, 2] = m
        for d in range(3):
            prep[slot, 3 + d] = m * vel[d, rr, :]
        prep[slot, 6] = jnp.where(top, 0.0, w[0])
        prep[slot, 7] = jnp.where(top, w[0], w[1])
        prep[slot, 8] = jnp.where(top, w[1], w[2])
        prep[slot, 9] = jnp.where(top, w[2], 0.0)
        return [first[2 * j, 0] for j in range(UR // 2)], jnp.where(live, yrel, 0)

    def build(i, slot, unit, j):
        row = urow[unit]
        for k in range(2):
            r = 2 * j + k

            def wide(tile):
                return jnp.broadcast_to(tile, (16, 128)).astype(BF)

            def own(q):
                return wide(prep[slot, q, r:r + 1, :])

            def weight(q):
                return wide(wt[q, pl.ds(row + r, 1), :])

            def taps(index, con, w):
                tile = jnp.where(index == con[0], w[0], zero)
                tile = jnp.where(index == con[1], w[1], tile)
                return jnp.where(index == con[2], w[2], tile)

            lanes = slice(k * 128, (k + 1) * 128)
            xw = taps(own(1), xcon, [weight(3 + p) for p in range(3)])
            for z in range(4):
                lbuf[i, z * 16:(z + 1) * 16, lanes] = own(6 + z) * xw
            wy = [weight(6 + t) for t in range(3)]
            yb = own(0)
            ya, yz = taps(yb, ycon, wy), taps(yb, ycon_b, wy)
            cb = [own(2 + f) for f in range(4)]
            for f in range(4):
                rbuf[i, f * 16:(f + 1) * 16, lanes] = cb[f] * ya
            for h in range(2):
                rbuf[i, 64 + h * 16:80 + h * 16, lanes] = jnp.where(upper, cb[2 * h], cb[2 * h + 1]) * yz

    def multiply(i, b, base):
        res = lax.dot_general(rbuf[i], lbuf[i], (((1,), (1,)), ((), ())), preferred_element_type=F32)
        for f in range(4):
            acc[b, f, pl.ds(pl.multiple_of(base, 8), 16), 0:64] += res[16 * f:16 * f + 16]
            acc[b, f, pl.ds(pl.multiple_of(base + 16, 8), 8), 0:64] += res[64 + 8 * f:72 + 8 * f]

    def turn(b):
        for h in range(2):
            def rows(f):
                head = acc[b, f, 1:9] + jnp.where(sub == 0, acc[b, f, 129:137], 0.0)
                tail = acc[b, f, 121:129] + jnp.where(sub == 7, jnp.broadcast_to(acc[b, f, 0:1], (8, 128)), 0.0)
                return jnp.concatenate([head, acc[b, f, 9:121], tail], 0)
            tbuf[b, h] = (rows(2 * h) + pltpu.roll(rows(2 * h + 1), 64, 1)).T

    def group(g, state):
        t, far_before = state
        at = g * U
        more = jnp.max(far_before) >= W - 2
        far = None
        if XP and ORDER == 0:
            for k in range(XP):
                turn(jnp.minimum(t + k, BLOCKS - 1))
        for k in range(U):
            if XP and ORDER == 1 and k % (U // XP) == 0:
                turn(jnp.minimum(t + k // (U // XP), BLOCKS - 1))
            for j in range(UR // 2):
                i = k * (UR // 2) + j
                multiply(i, urow[at + k] // ROWS, ubase[2 * at + i])
                build(i, k, at + U + k, j)
            bases, spread = prepare(k, at + 2 * U + k)
            for j in range(UR // 2):
                ubase[2 * (at + 2 * U) + k * (UR // 2) + j] = bases[j]
            far = spread if far is None else jnp.maximum(far, spread)

        if XP:
            t = jnp.maximum(t, jnp.minimum(t + XP, urow[at] // ROWS))

        @pl.when(more)
        def _():
            def one(k, _):
                unit = at + U + k
                b = urow[unit] // ROWS
                prepare(U, unit)

                def window(off, _):
                    prep[U, 0] = prep[U, 0] - float(W)
                    for j in range(UR // 2):
                        base = ubase[2 * unit + j] + off * W

                        @pl.when(base < 130)
                        def _():
                            build(chunks, U, unit, j)
                            multiply(chunks, b, base)
                    return 0

                lax.fori_loop(1, 6, window, 0)
                return 0

            lax.fori_loop(0, U, one, 0)

        return t, far

    for c in copies(0):
        c.wait()
    head_groups = (head_end - 2 * U) // U
    state = lax.fori_loop(0, head_groups, group, (0, jnp.zeros((UR, 128), jnp.int32)))
    for c in copies(1):
        c.wait()
    t, _ = lax.fori_loop(head_groups, (end + U - 1) // U, group, state)

    def rest(k, _):
        for j in range(4):
            turn(jnp.minimum(t + 4 * k + j, BLOCKS - 1))
        return 0

    lax.fori_loop(0, (BLOCKS - t + 3) // 4, rest, 0)

    def piece(p):
        return pltpu.make_async_copy(obuf.at[p], out.at[p], out_sem.at[p])

    def seams(p, _):
        for j in range(4):
            b = p * 4 + j
            dn = (b + BLOCKS - 1) & (BLOCKS - 1)
            up = (b + 1) & (BLOCKS - 1)
            for k in range(16):
                o = (k // 4 % 2) * 64 + k % 4 * 16
                h = k // 8
                obuf[p, k, 8 * j:8 * j + 8, :] = (
                    tbuf[b, h, o:o + 8]
                    + jnp.where(sub == 0, tbuf[dn, h, o + 8:o + 16], 0.0)
                    + jnp.where(sub == 7, tbuf[up, h, o + 8:o + 16], 0.0))
        piece(p).start()
        return 0

    lax.fori_loop(0, 8, seams, 0)

    def drain_out(p, _):
        piece(p).wait()
        return 0

    lax.fori_loop(0, 8, drain_out, 0)


def deposit(cfg, counts, mass, vel, wt, cells):
    U, XP, ORDER = cfg
    chunks = U * UR // 2
    hbm = pl.BlockSpec(memory_space=pltpu.MemorySpace.HBM)
    units = BLOCKS * PER_BLOCK + 5 * U + PER_BLOCK
    return pl.pallas_call(
        functools.partial(deposit_kernel, U, XP, ORDER),
        in_specs=[pl.BlockSpec(memory_space=pltpu.SMEM), hbm, hbm, hbm, hbm],
        out_specs=hbm,
        out_shape=jax.ShapeDtypeStruct((112, 16, 32, 128), F32),
        scratch_shapes=[
            pltpu.VMEM((1024, 128), F32), pltpu.VMEM((3, 1024, 128), F32), pltpu.VMEM((9, 1024, 128), F32),
            pltpu.VMEM((1024, 128), jnp.int32), pltpu.VMEM((BLOCKS, 4, 160, 128), F32),
            pltpu.VMEM((BLOCKS, 2, 128, 128), F32), pltpu.VMEM((U + 1, 10, UR, 128), F32),
            pltpu.VMEM((chunks + 1, 64, 256), BF), pltpu.VMEM((chunks + 1, 4 * W, 256), BF),
            pltpu.VMEM((8, 16, 32, 128), F32),
            pltpu.SMEM((units,), jnp.int32), pltpu.SMEM((units,), jnp.int32), pltpu.SMEM((2 * units,), jnp.int32),
            pltpu.SemaphoreType.DMA((4, 2)), pltpu.SemaphoreType.DMA((8,)),
        ],
        compiler_params=pltpu.CompilerParams(vmem_limit_bytes=60 << 20),
    )(counts, mass.reshape(1024, 128), vel.reshape(3, 1024, 128), wt.reshape(9, 1024, 128), cells.reshape(1024, 128))


MASS_FLOOR = 0.2
GRADIENT_FLOOR = 0.1
SLIP_FLOOR = 0.05
PIECES = 8
COLS = 32
MID = 7
MESH = pl.DeviceIdType.MESH


def comm_kernel(fric, dep_h, flags_h, out, dep, flags, d_s, f_s, hsend, hrecv, msend, mrecv, nf, mass, rsend, rrecv, ysend,
                yrecv, cbuf, h_ss, h_rs, m_ss, m_rs, r_ss, r_rs, y_ss, y_rs, c_ss, c_rs):
    slabs = lax.axis_size("gz")
    g = lax.axis_index("gz")
    me = lax.axis_index("mat")
    lo = lax.rem(g + slabs - 1, slabs)
    hi = lax.rem(g + 1, slabs)
    s_lo = jnp.where(g == 0, 0.0, 1.0)
    s_hi = jnp.where(g == slabs - 1, 0.0, 1.0)

    def fetch(p):
        return pltpu.make_async_copy(dep_h.at[p], dep.at[p], d_s.at[p])

    def start_fetch(k, _):
        fetch(lax.rem(me + 1 + k, PIECES)).start()
        return 0

    lax.fori_loop(0, PIECES, start_fetch, 0)
    fetch_flags = pltpu.make_async_copy(flags_h, flags, f_s)
    fetch_flags.start()

    barrier = pltpu.get_barrier_semaphore()
    for other in (lo, hi):
        pl.semaphore_signal(barrier, inc=1, device_id={"gz": other, "mat": me}, device_id_type=MESH)
    for k in range(1, PIECES):
        pl.semaphore_signal(barrier, inc=1, device_id={"gz": g, "mat": lax.rem(me + k, PIECES)},
                            device_id_type=MESH)

    def halo(side, p):
        return pltpu.make_async_remote_copy(
            src_ref=hsend.at[side, p], dst_ref=hrecv.at[side, p],
            send_sem=h_ss.at[side, p], recv_sem=h_rs.at[side, p],
            device_id={"gz": lo if side == 0 else hi, "mat": me}, device_id_type=MESH)

    x_me = me // 2
    y_me = me % 2

    def order(k):
        return lax.rem(x_me + 1 + k, 4) * 2 + jnp.where(k < 4, 1 - y_me, y_me)

    def edge(side):
        return pltpu.make_async_remote_copy(
            src_ref=msend.at[side], dst_ref=mrecv.at[side], send_sem=m_ss.at[side], recv_sem=m_rs.at[side],
            device_id={"gz": lo if side == 0 else hi, "mat": me}, device_id_type=MESH)

    def share(k):
        half = k // 4
        return pltpu.make_async_remote_copy(
            src_ref=rsend.at[order(k)], dst_ref=rrecv.at[half, x_me], send_sem=r_ss.at[k],
            recv_sem=r_rs.at[half, x_me],
            device_id={"gz": g, "mat": lax.rem(x_me + 1 + k, 4) * 2 + y_me}, device_id_type=MESH)

    def shared(half, x):
        return pltpu.make_async_remote_copy(
            src_ref=rsend.at[0], dst_ref=rrecv.at[half, x], send_sem=r_ss.at[0], recv_sem=r_rs.at[half, x],
            device_id={"gz": g, "mat": x * 2 + y_me}, device_id_type=MESH)

    def cross():
        return pltpu.make_async_remote_copy(
            src_ref=ysend, dst_ref=yrecv, send_sem=y_ss, recv_sem=y_rs,
            device_id={"gz": g, "mat": x_me * 2 + 1 - y_me}, device_id_type=MESH)

    def spread(p):
        return pltpu.make_async_remote_copy(
            src_ref=cbuf.at[me], dst_ref=cbuf.at[me], send_sem=c_ss.at[p], recv_sem=c_rs.at[me],
            device_id={"gz": g, "mat": p}, device_id_type=MESH)

    def spreaded(p):
        return pltpu.make_async_remote_copy(
            src_ref=cbuf.at[p], dst_ref=cbuf.at[p], send_sem=c_ss.at[p], recv_sem=c_rs.at[p],
            device_id={"gz": g, "mat": p}, device_id_type=MESH)

    def cols(p):
        return pl.ds(pl.multiple_of(p * COLS, COLS), COLS)

    def pack(k, _):
        p = order(k)
        fetch(p).wait()
        for f in range(4):
            hsend[0, p, f] = dep[p, 4 * f + 0].astype(jnp.bfloat16)
            hsend[1, p, f] = dep[p, 4 * f + 3].astype(jnp.bfloat16)
        msend[0, cols(p), :] = dep[p, 1].astype(jnp.bfloat16)
        msend[1, cols(p), :] = dep[p, 2].astype(jnp.bfloat16)
        return 0

    lax.fori_loop(0, PIECES, pack, 0)
    pl.semaphore_wait(barrier, PIECES + 1)

    def start_halo(k, _):
        p = order(k)
        halo(0, p).start()
        halo(1, p).start()
        return 0

    lax.fori_loop(0, PIECES, start_halo, 0)
    edge(0).start()
    edge(1).start()

    def nodes(p):
        halo(0, p).wait_recv()
        halo(1, p).wait_recv()
        x = cols(p)
        for f in range(4):
            low = dep[p, 4 * f + 1] + s_lo * hrecv[1, p, f].astype(jnp.float32)
            high = dep[p, 4 * f + 2] + s_hi * hrecv[0, p, f].astype(jnp.float32)
            nf[f, 0, x, :] = low
            nf[f, 1, x, :] = high
            rsend[p, f, 0] = low.astype(jnp.bfloat16)
            rsend[p, f, 1] = high.astype(jnp.bfloat16)
            if f == 0:
                xm = pl.ds(pl.multiple_of(p * COLS + 8, 8), COLS)
                mass[0, xm, :] = low
                mass[1, xm, :] = high

    def reduce_step(k, _):
        nodes(order(k))
        share(k).start()
        return 0

    def total_step(half):
        def step(k, total):
            x = lax.rem(x_me + 3 - k, 4)
            shared(half, x).wait_recv()
            return total + rrecv[half, x].astype(jnp.float32)
        own = rsend[order(4 * half + 3)].astype(jnp.float32)
        return lax.fori_loop(0, 3, step, own)

    lax.fori_loop(0, 3, reduce_step, 0)
    nodes(order(3))
    lax.fori_loop(4, MID, reduce_step, 0)
    ysend[...] = total_step(0).astype(jnp.bfloat16)
    cross().start()
    lax.fori_loop(MID, 7, reduce_step, 0)
    nodes(me)
    for z in range(2):
        mass[z, 7:8, :] = mass[z, 263:264, :]
        mass[z, 264:265, :] = mass[z, 8:9, :]

    total = total_step(1)
    cross().wait_recv()
    total = total + yrecv[...].astype(jnp.float32)
    cbuf[me] = (total[1:] / jnp.maximum(total[0], MASS_FLOOR)).astype(jnp.bfloat16)

    def start_spread(k, _):
        spread(lax.rem(me + 1 + k, PIECES)).start()
        return 0

    lax.fori_loop(0, PIECES - 1, start_spread, 0)
    friction = fric[0]
    fetch_flags.wait()
    edge(0).wait_recv()
    edge(1).wait_recv()

    def finish(p):
        for z in range(2):
            x = cols(p)
            m = nf[0, z, x, :]
            gx = (mass[z, pl.ds(p * COLS + 9, COLS), :] - mass[z, pl.ds(p * COLS + 7, COLS), :]) * 0.5
            gy = (pltpu.roll(m, 127, 1) - pltpu.roll(m, 1, 1)) * 0.5
            if z == 0:
                below = s_lo * (mrecv[1, x, :].astype(jnp.float32) + dep[p, 0])
                gz = (nf[0, 1, x, :] - below) * 0.5
            else:
                above = s_hi * (mrecv[0, x, :].astype(jnp.float32) + dep[p, 3])
                gz = (above - nf[0, 0, x, :]) * 0.5
            length = jnp.sqrt(gz * gz + gx * gx + gy * gy)
            inv = 1.0 / jnp.maximum(length, GRADIENT_FLOOR)
            normal = [gz * inv, gx * inv, gy * inv]
            inv_m = 1.0 / jnp.maximum(m, MASS_FLOOR)
            speed = [nf[1 + d, z, x, :] * inv_m for d in range(3)]
            rel = [speed[d] - cbuf[p, d, z].astype(jnp.float32) for d in range(3)]
            part = rel[0] * normal[0] + rel[1] * normal[1] + rel[2] * normal[2]
            approach = jnp.maximum(part, 0.0)
            tangent = [rel[d] - part * normal[d] for d in range(3)]
            slip = jnp.sqrt(tangent[0] * tangent[0] + tangent[1] * tangent[1] + tangent[2] * tangent[2])
            factor = jnp.minimum(friction * approach, slip) / jnp.maximum(slip, SLIP_FLOOR)
            flag = flags[z, x, :].astype(jnp.float32)
            for d in range(3):
                out[0, d, z, x, :] = speed[d] - flag * (approach * normal[d] + factor * tangent[d])

    finish(me)
    def finish_step(k, _):
        p = lax.rem(me + PIECES - 1 - k, PIECES)
        spreaded(p).wait_recv()
        finish(p)
        return 0

    lax.fori_loop(0, PIECES - 1, finish_step, 0)

    def drain(k, _):
        p = lax.rem(me + 1 + k, PIECES)
        spread(p).wait_send()
        return 0

    lax.fori_loop(0, PIECES - 1, drain, 0)

    def drain_share(k, _):
        share(k).wait_send()
        share(k + 4).wait_send()
        return 0

    lax.fori_loop(0, 3, drain_share, 0)
    cross().wait_send()
    edge(0).wait_send()
    edge(1).wait_send()

    def drain_halo(p, _):
        halo(0, p).wait_send()
        halo(1, p).wait_send()
        return 0

    lax.fori_loop(0, PIECES, drain_halo, 0)


def exchange(friction, dep, flags):
    hbm = pl.BlockSpec(memory_space=pltpu.MemorySpace.HBM)
    f32, bf = jnp.float32, jnp.bfloat16
    dma = pltpu.SemaphoreType.DMA
    return pl.pallas_call(
        comm_kernel,
        in_specs=[pl.BlockSpec(memory_space=pltpu.SMEM), hbm, hbm],
        out_specs=pl.BlockSpec(memory_space=pltpu.VMEM),
        out_shape=jax.ShapeDtypeStruct((1, 3, 2, 256, 128), f32),
        scratch_shapes=[
            pltpu.VMEM((PIECES, 16, COLS, 128), f32), pltpu.VMEM((2, 256, 128), jnp.int32),
            dma((PIECES,)), dma,
            pltpu.VMEM((2, PIECES, 4, COLS, 128), bf), pltpu.VMEM((2, PIECES, 4, COLS, 128), bf),
            pltpu.VMEM((2, 256, 128), bf), pltpu.VMEM((2, 256, 128), bf),
            pltpu.VMEM((4, 2, 256, 128), f32), pltpu.VMEM((2, 272, 128), f32),
            pltpu.VMEM((PIECES, 4, 2, COLS, 128), bf), pltpu.VMEM((2, 4, 4, 2, COLS, 128), bf),
            pltpu.VMEM((4, 2, COLS, 128), bf), pltpu.VMEM((4, 2, COLS, 128), bf),
            pltpu.VMEM((PIECES, 3, 2, COLS, 128), bf),
            dma((2, PIECES)), dma((2, PIECES)), dma((2,)), dma((2,)), dma((PIECES,)), dma((2, 4)),
            dma, dma, dma((PIECES,)), dma((PIECES,)),
        ],
        compiler_params=pltpu.CompilerParams(collective_id=0, has_side_effects=True, vmem_limit_bytes=40 << 20),
    )(friction, dep, flags)


def per_device(particle_mass, particle_velocity, spline_weights, particle_cells, block_counts, friction, contact_flags):
    dep = deposit((8, 2, 0), block_counts.reshape(32), particle_mass, particle_velocity, spline_weights, particle_cells)
    return exchange(friction, dep, contact_flags)


def solution(mesh):
    return jax.shard_map(
        per_device,
        mesh=mesh,
        in_specs=(
            P("mat", "gz"),
            P("mat", None, "gz"),
            P("mat", None, "gz"),
            P("mat", "gz"),
            P("mat", "gz", None),
            P("mat"),
            P("gz", None, None),
        ),
        out_specs=P("mat", None, "gz", None, None),
        check_vma=False,
    )
```

time: 58.4 us -> 51.1 us (0.88)
  the two profiles are of different devices: /device:TPU:40 before, /device:TPU:16 now
where the time goes in v3:
time: 51.1 us; the launch traced here: 51 us
  Pallas kernels  49.4 us (97%)
  local copies, waits for them, and re-layouts  0.89 us (2%)
  between operations  0.68 us (1%)
    pallas_call x1, Pallas kernels, exchange(): pl.pallas_call(comm_kernel, in_specs=[pl.BlockSpec(memory_space=pltpu.SME...  28.9 us
    pallas_call x1, Pallas kernels, deposit(): pl.pallas_call(functools.partial(deposit_kernel, U, XP, ORDER), in_specs=...  20.5 us

profile of v3, /device:TPU:16, one launch (start us, length us, event | category | flops | bytes accessed | tf_op | source)
XLA Modules:
  0.0 51.0 jit_solution(6529919648029810521)
XLA Ops:
  0.7 0.0 copy-start
  0.7 20.5 %shard_map.73.dep_h = f32[112,16,32,128]{3,2,1,0:T(8,128)} custom-call(s32[32]{0:T(128)} %bitcast.9, f32[1024,128]{1,0:T(8,128)} %bitcast.7, f32[3,1024,128]{2,1,0:T(8,128)} %bitcast.6, f32[9,1024,128]{2,1,0:T(8,128)} %bitcast.5, s32[1024,128]{1,0:T(8,128)} %bitcast.8), custom_call_target="tpu_custom_call" | custom-call | tf_op jit(solution)/shard_map/pallas_call | solution.py:246
  21.1 0.0 copy-done
  21.2 28.9 %shard_map.74 = f32[1,3,2,256,128]{4,3,2,1,0:T(8,128)S(1)} custom-call(f32[1]{0:T(128)S(6)} %copy.9.fric, f32[112,16,32,128]{3,2,1,0:T(8,128)} %shard_map.73.dep_h, s32[2,256,128]{2,1,0:T(8,128)S(1)} %copy-done), custom_call_target="tpu_custom_call" | custom-call | tf_op jit(solution)/shard_map/pallas_call | solution.py:491
  50.1 0.9 %copy.10 = f32[1,3,2,256,128]{4,3,2,1,0:T(8,128)} copy(f32[1,3,2,256,128]{4,3,2,1,0:T(8,128)S(1)} %shard_map.74) | data formatting | bytes 1572864
Async XLA Ops:
  0.7 20.5 %copy-start = (s32[2,256,128]{2,1,0:T(8,128)S(1)}, s32[2,256,128]{2,1,0:T(8,128)}, u32[]{:S(2)}) copy-start(s32[2,256,128]{2,1,0:T(8,128)} %flags_h.1) | copy-start | bytes 786436

commit v4 on v3

--- a/solution.py
+++ b/solution.py
@@ -47,6 +47,7 @@
     ycon_b = [const(16 + (row16 & 7) - t) for t in range(3)]
     upper = const(row16) < jnp.asarray(8, BF)
     zero = jnp.zeros((), BF)
+    one = jnp.ones((), BF)
 
     def dead(i, row):
         urow[i] = row
@@ -93,13 +94,11 @@
         w = [wt[a, rr, :] for a in range(3)]
         prep[slot, 0] = yrel.astype(F32)
         prep[slot, 1] = ((cl >> 7) & 7).astype(F32)
-        prep[slot, 2] = m
-        for d in range(3):
-            prep[slot, 3 + d] = m * vel[d, rr, :]
-        prep[slot, 6] = jnp.where(top, 0.0, w[0])
-        prep[slot, 7] = jnp.where(top, w[0], w[1])
-        prep[slot, 8] = jnp.where(top, w[1], w[2])
-        prep[slot, 9] = jnp.where(top, w[2], 0.0)
+        w = [m * v for v in w]
+        prep[slot, 2] = jnp.where(top, 0.0, w[0])
+        prep[slot, 3] = jnp.where(top, w[0], w[1])
+        prep[slot, 4] = jnp.where(top, w[1], w[2])
+        prep[slot, 5] = jnp.where(top, w[2], 0.0)
         return [first[2 * j, 0] for j in range(UR // 2)], jnp.where(live, yrel, 0)
 
     def build(i, slot, unit, j):
@@ -124,15 +123,16 @@
             lanes = slice(k * 128, (k + 1) * 128)
             xw = taps(own(1), xcon, [weight(3 + p) for p in range(3)])
             for z in range(4):
-                lbuf[i, z * 16:(z + 1) * 16, lanes] = own(6 + z) * xw
+                lbuf[i, z * 16:(z + 1) * 16, lanes] = own(2 + z) * xw
             wy = [weight(6 + t) for t in range(3)]
             yb = own(0)
             ya, yz = taps(yb, ycon, wy), taps(yb, ycon_b, wy)
-            cb = [own(2 + f) for f in range(4)]
-            for f in range(4):
-                rbuf[i, f * 16:(f + 1) * 16, lanes] = cb[f] * ya
-            for h in range(2):
-                rbuf[i, 64 + h * 16:80 + h * 16, lanes] = jnp.where(upper, cb[2 * h], cb[2 * h + 1]) * yz
+            v = [wide(vel[d, pl.ds(row + r, 1), :]) for d in range(3)]
+            rbuf[i, 0:16, lanes] = ya
+            for d in range(3):
+                rbuf[i, (d + 1) * 16:(d + 2) * 16, lanes] = v[d] * ya
+            rbuf[i, 64:80, lanes] = jnp.where(upper, one, v[0]) * yz
+            rbuf[i, 80:96, lanes] = jnp.where(upper, v[1], v[2]) * yz
 
     def multiply(i, b, base):
         res = lax.dot_general(rbuf[i], lbuf[i], (((1,), (1,)), ((), ())), preferred_element_type=F32)
@@ -173,7 +173,7 @@
 
         @pl.when(more)
         def _():
-            def one(k, _):
+            def again(k, _):
                 unit = at + U + k
                 b = urow[unit] // ROWS
                 prepare(U, unit)
@@ -192,7 +192,7 @@
                 lax.fori_loop(1, 6, window, 0)
                 return 0
 
-            lax.fori_loop(0, U, one, 0)
+            lax.fori_loop(0, U, again, 0)
 
         return t, far
 
@@ -251,7 +251,7 @@
         scratch_shapes=[
             pltpu.VMEM((1024, 128), F32), pltpu.VMEM((3, 1024, 128), F32), pltpu.VMEM((9, 1024, 128), F32),
             pltpu.VMEM((1024, 128), jnp.int32), pltpu.VMEM((BLOCKS, 4, 160, 128), F32),
-            pltpu.VMEM((BLOCKS, 2, 128, 128), F32), pltpu.VMEM((U + 1, 10, UR, 128), F32),
+            pltpu.VMEM((BLOCKS, 2, 128, 128), F32), pltpu.VMEM((U + 1, 6, UR, 128), F32),
             pltpu.VMEM((chunks + 1, 64, 256), BF), pltpu.VMEM((chunks + 1, 4 * W, 256), BF),
             pltpu.VMEM((8, 16, 32, 128), F32),
             pltpu.SMEM((units,), jnp.int32), pltpu.SMEM((units,), jnp.int32), pltpu.SMEM((2 * units,), jnp.int32),
@@ -365,8 +365,6 @@
         return 0
 
     lax.fori_loop(0, PIECES, start_halo, 0)
-    edge(0).start()
-    edge(1).start()
 
     def nodes(p):
         halo(0, p).wait_recv()
@@ -402,6 +400,8 @@
     lax.fori_loop(4, MID, reduce_step, 0)
     ysend[...] = total_step(0).astype(jnp.bfloat16)
     cross().start()
+    edge(0).start()
+    edge(1).start()
     lax.fori_loop(MID, 7, reduce_step, 0)
     nodes(me)
     for z in range(2):
@@ -427,16 +427,15 @@
         for z in range(2):
             x = cols(p)
             m = nf[0, z, x, :]
-            gx = (mass[z, pl.ds(p * COLS + 9, COLS), :] - mass[z, pl.ds(p * COLS + 7, COLS), :]) * 0.5
-            gy = (pltpu.roll(m, 127, 1) - pltpu.roll(m, 1, 1)) * 0.5
+            gx = mass[z, pl.ds(p * COLS + 9, COLS), :] - mass[z, pl.ds(p * COLS + 7, COLS), :]
+            gy = pltpu.roll(m, 127, 1) - pltpu.roll(m, 1, 1)
             if z == 0:
                 below = s_lo * (mrecv[1, x, :].astype(jnp.float32) + dep[p, 0])
-                gz = (nf[0, 1, x, :] - below) * 0.5
+                gz = nf[0, 1, x, :] - below
             else:
                 above = s_hi * (mrecv[0, x, :].astype(jnp.float32) + dep[p, 3])
-                gz = (above - nf[0, 0, x, :]) * 0.5
-            length = jnp.sqrt(gz * gz + gx * gx + gy * gy)
-            inv = 1.0 / jnp.maximum(length, GRADIENT_FLOOR)
+                gz = above - nf[0, 0, x, :]
+            inv = lax.rsqrt(jnp.maximum(gz * gz + gx * gx + gy * gy, 4.0 * GRADIENT_FLOOR * GRADIENT_FLOOR))
             normal = [gz * inv, gx * inv, gy * inv]
             inv_m = 1.0 / jnp.maximum(m, MASS_FLOOR)
             speed = [nf[1 + d, z, x, :] * inv_m for d in range(3)]
@@ -444,8 +443,9 @@
             part = rel[0] * normal[0] + rel[1] * normal[1] + rel[2] * normal[2]
             approach = jnp.maximum(part, 0.0)
             tangent = [rel[d] - part * normal[d] for d in range(3)]
-            slip = jnp.sqrt(tangent[0] * tangent[0] + tangent[1] * tangent[1] + tangent[2] * tangent[2])
-            factor = jnp.minimum(friction * approach, slip) / jnp.maximum(slip, SLIP_FLOOR)
+            slip2 = tangent[0] * tangent[0] + tangent[1] * tangent[1] + tangent[2] * tangent[2]
+            slip = slip2 * lax.rsqrt(jnp.maximum(slip2, 1.2e-38))
+            factor = jnp.minimum(friction * approach, slip) * lax.rsqrt(jnp.maximum(slip2, SLIP_FLOOR * SLIP_FLOOR))
             flag = flags[z, x, :].astype(jnp.float32)
             for d in range(3):
                 out[0, d, z, x, :] = speed[d] - flag * (approach * normal[d] + factor * tangent[d])

time: 51.1 us -> 50 us (0.978)
  Pallas kernels: 49.4 us -> 48.3 us
    pallas_call x1, Pallas kernels: 20.5 us -> 13.8 us  [deposit(): pl.pallas_call(functools.partial(deposit_kernel, U, XP, ORDER), in_specs=...]
    pallas_call x1, Pallas kernels: 28.9 us -> 34.4 us  [exchange(): pl.pallas_call(comm_kernel, in_specs=[pl.BlockSpec(memory_space=pltpu.SME...]
where the time goes in v4:
time: 50 us; the launch traced here: 49.8 us
  Pallas kernels  48.3 us (97%)
  local copies, waits for them, and re-layouts  0.89 us (2%)
  between operations  0.68 us (1%)
    pallas_call x1, Pallas kernels, exchange(): pl.pallas_call(comm_kernel, in_specs=[pl.BlockSpec(memory_space=pltpu.SME...  34.4 us
    pallas_call x1, Pallas kernels, deposit(): pl.pallas_call(functools.partial(deposit_kernel, U, XP, ORDER), in_specs=...  13.8 us

profile of v4, /device:TPU:16, one launch (start us, length us, event | category | flops | bytes accessed | tf_op | source)
XLA Modules:
  0.0 49.8 jit_solution(12229037948749530493)
XLA Ops:
  0.7 0.0 copy-start
  0.7 13.8 %shard_map.73.dep_h = f32[112,16,32,128]{3,2,1,0:T(8,128)} custom-call(s32[32]{0:T(128)} %bitcast.9, f32[1024,128]{1,0:T(8,128)} %bitcast.7, f32[3,1024,128]{2,1,0:T(8,128)} %bitcast.6, f32[9,1024,128]{2,1,0:T(8,128)} %bitcast.5, s32[1024,128]{1,0:T(8,128)} %bitcast.8), custom_call_target="tpu_custom_call" | custom-call | tf_op jit(solution)/shard_map/pallas_call | solution.py:246
  14.5 0.0 copy-done
  14.5 34.4 %shard_map.74 = f32[1,3,2,256,128]{4,3,2,1,0:T(8,128)S(1)} custom-call(f32[1]{0:T(128)S(6)} %copy.9.fric, f32[112,16,32,128]{3,2,1,0:T(8,128)} %shard_map.73.dep_h, s32[2,256,128]{2,1,0:T(8,128)S(1)} %copy-done), custom_call_target="tpu_custom_call" | custom-call | tf_op jit(solution)/shard_map/pallas_call | solution.py:491
  48.9 0.9 %copy.10 = f32[1,3,2,256,128]{4,3,2,1,0:T(8,128)} copy(f32[1,3,2,256,128]{4,3,2,1,0:T(8,128)S(1)} %shard_map.74) | data formatting | bytes 1572864
Async XLA Ops:
  0.7 13.8 %copy-start = (s32[2,256,128]{2,1,0:T(8,128)S(1)}, s32[2,256,128]{2,1,0:T(8,128)}, u32[]{:S(2)}) copy-start(s32[2,256,128]{2,1,0:T(8,128)} %flags_h.1) | copy-start | bytes 786436
